TPU v7x, 128 devices: a whole 4x4x4 slice. The times are simulated.
128 devices in a mesh: group: 4 (over y), fsdp: 8 (over x_lo, z), tp: 4 (over x_hi, core).
Axes of the slice: x: 4 (x_hi: 2, x_lo: 2; x = x_hi * 2 + x_lo), y: 4, z: 4, core: 2. Of those that a mesh axis runs over, the one named last changes fastest.
Arguments:
- noise_in: bfloat16 [256, 5120], P('fsdp'), may hold values from -6 to 6
- noise: bfloat16 [256, 5120], P('fsdp'), may hold values from -6 to 6
- timesteps: int32 [8], P('fsdp'), may hold values from 20 to 979
- up_weight: bfloat16 [4, 6912, 5120], P('group', ('fsdp', 'tp')), may hold values from -0.078125 to 0.078125
- down_weight: bfloat16 [4, 6912, 5120], P('group', ('fsdp', 'tp')), may hold values from -0.0546875 to 0.0546875
- small_params: float32 [3, 5, 5120], replicated, may hold values from -3 to 3
Outputs:
- score_gap: float32 [256, 5120], P('fsdp')
- up_grads: float32 [4, 6912, 5120], P('group', ('fsdp', 'tp'))
- down_grads: float32 [4, 6912, 5120], P('group', ('fsdp', 'tp'))
- small_grads: float32 [4, 5, 5120], P('group', None, ('fsdp', 'tp'))
All inputs are finite; a program needn't handle non-finite values.
Results may differ from a plain program's by a relative error of at most 0.019.
Values may be sent and summed in bfloat16 or wider, within the bound.
A program may use at most 128 MiB of HBM per device.

v0:
```python
import math

import jax
import jax.numpy as jnp
from jax import lax
from jax.sharding import PartitionSpec as P

gen_time = 999.0
epsilon_norm = 1e-06
epsilon_gap = 1e-05


def partner_2(value, axis, apart):
    mask = 2**apart
    pairs = [(source, source ^ mask) for source in range(lax.axis_size(axis))]
    return lax.ppermute(value, axis, pairs)


def shifted(value, axis, steps):
    count = lax.axis_size(axis)
    initial, last = (max(0, -steps), min(count, count - steps))
    return lax.ppermute(value, axis, [(source, source + steps) for source in range(initial, last)])


def gelu_tanh(inputs):
    return jax.nn.gelu(inputs, approximate=True)


def embedding(step_value, feature_width):
    half_width = feature_width // 2
    freqs = jnp.exp(-math.log(10000.0) * jnp.arange(half_width, dtype=jnp.float32) / half_width)
    angles = step_value * freqs
    return jnp.concatenate([jnp.cos(angles), jnp.sin(angles)], axis=-1)


def hidden_total(term_fn, row_count, is_pair):
    shared = lax.psum_scatter(
        term_fn(jnp.int32(0), row_count // lax.axis_size("tp") * lax.axis_size(("fsdp", "tp"))),
        ("fsdp", "tp"),
        scatter_dimension=0,
        tiled=True,
    )
    partner = partner_2(shared, "group", 0)
    shared = shared + jnp.where(is_pair, partner, 0.0)
    shared, partner = (
        lax.all_gather(shared, "tp", axis=0, tiled=True),
        lax.all_gather(partner, "tp", axis=0, tiled=True),
    )
    return (shared, partner)


def forward_block(inputs, time_vec, params, up_rows, down_rows, is_pair):
    values = inputs.astype(jnp.float32)
    center = jnp.mean(values, axis=1, keepdims=True)
    spread = jnp.mean(jnp.square(values - center), axis=1, keepdims=True)
    normed = (values - center) * lax.rsqrt(spread + epsilon_norm)
    layered = normed * (1.0 + params[0]) + params[1]
    scale_vec = params[3] + time_vec
    shift_vec = params[2] + time_vec
    gate_vec = params[4] + time_vec
    modulated = (layered * (1.0 + scale_vec) + shift_vec).astype(jnp.bfloat16)
    all_rows = lax.all_gather(modulated, "fsdp", axis=0, tiled=True)
    hidden_pre = lax.dot_general(
        up_rows, all_rows, (((1,), (1,)), ((), ())), preferred_element_type=jnp.float32
    )
    active = gelu_tanh(hidden_pre).astype(jnp.bfloat16)

    def term_fn(offset, amount):
        return lax.dot_general(
            active, down_rows, (((0,), (0,)), ((), ())), preferred_element_type=jnp.float32
        )

    mixed_sum, partner_sum = hidden_total(term_fn, inputs.shape[0], is_pair)
    output = (values + gate_vec * mixed_sum).astype(jnp.bfloat16)
    return (
        output,
        partner_sum,
        (normed, layered, scale_vec, gate_vec, modulated, all_rows, hidden_pre, active, mixed_sum),
    )


def backward_block(cotangent, saved, up_rows, down_rows, is_pair):
    normed, layered, scale_vec, gate_vec, modulated, all_rows, hidden_pre, active, mixed_sum = saved
    gate_grad = jnp.sum(cotangent * mixed_sum, axis=0)
    mixed_grad = (cotangent * gate_vec).astype(jnp.bfloat16)
    mixed_rows = lax.all_gather(mixed_grad, "fsdp", axis=0, tiled=True)
    active_grad = lax.dot_general(
        down_rows, mixed_rows, (((1,), (1,)), ((), ())), preferred_element_type=jnp.float32
    )
    hidden_grad = jax.vjp(gelu_tanh, hidden_pre)[1](active_grad)[0].astype(jnp.bfloat16)
    down_grad = jnp.dot(active, mixed_rows, preferred_element_type=jnp.float32)
    up_grad = jnp.dot(hidden_grad, all_rows, preferred_element_type=jnp.float32)

    def term_fn(offset, amount):
        return lax.dot_general(
            hidden_grad, up_rows, (((0,), (0,)), ((), ())), preferred_element_type=jnp.float32
        )

    input_grad, unused_sum = hidden_total(term_fn, cotangent.shape[0], is_pair)
    layer_grad = input_grad * (1.0 + scale_vec)
    stacked = jnp.stack(
        [
            jnp.sum(layer_grad * normed, axis=0),
            jnp.sum(layer_grad, axis=0),
            jnp.sum(input_grad, axis=0),
            jnp.sum(input_grad * layered, axis=0),
            gate_grad,
        ]
    )
    return (up_grad, down_grad, stacked)


def per_device(noise_in, noise, timesteps, up_weight, down_weight, small_params):
    group_index = lax.axis_index("group")
    is_gen = group_index < 2
    model_index = jnp.maximum(group_index - 1, 0)
    params = lax.dynamic_index_in_dim(small_params, model_index, 0, keepdims=False)
    other_index = jnp.clip(3 - model_index, 1, 2)
    other_params = lax.dynamic_index_in_dim(small_params, other_index, 0, keepdims=False)
    up_rows = up_weight[0]
    down_rows = down_weight[0]
    feature_width = noise_in.shape[1]
    latents = lax.axis_size("fsdp")
    gen_vec = embedding(jnp.float32(gen_time), feature_width)
    step_value = timesteps[0].astype(jnp.float32)
    data_vec = embedding(step_value, feature_width)
    first_out, unused_partner, first_saved = forward_block(
        noise_in, gen_vec, params, up_rows, down_rows, is_gen
    )
    arrived = shifted(first_out, "group", 2)
    samples = jnp.where(is_gen, first_out, arrived)
    sample_values = samples.astype(jnp.float32)
    noise_angle = 0.5 * math.pi * step_value / 1000.0
    noisy = (
        jnp.cos(noise_angle) * sample_values + jnp.sin(noise_angle) * noise.astype(jnp.float32)
    ).astype(jnp.bfloat16)
    second_out, other_sum, second_saved = forward_block(
        noisy, data_vec, params, up_rows, down_rows, is_gen
    )
    noisy_values = noisy.astype(jnp.float32)
    other_out = (noisy_values + (other_params[4] + data_vec) * other_sum).astype(jnp.bfloat16)
    is_teacher = group_index == 3
    fake_pred = jnp.where(is_teacher, other_out, second_out).astype(jnp.float32)
    real_pred = jnp.where(is_teacher, second_out, other_out).astype(jnp.float32)
    scale_gap = jnp.mean(jnp.abs(sample_values - real_pred)) + epsilon_gap
    gap_local = (fake_pred - real_pred) / scale_gap
    returned = shifted(gap_local, "group", -2)
    score_gap = jnp.where(is_gen, returned, gap_local)
    critic_cot = (fake_pred - sample_values) / latents
    cotangent = jnp.where(is_gen, score_gap / latents, jnp.where(group_index == 2, critic_cot, 0.0))
    saved = tuple(
        (
            jnp.where(is_gen, first_item, second_item)
            for first_item, second_item in zip(first_saved, second_saved)
        )
    )
    up_grad, down_grad, stacked = backward_block(cotangent, saved, up_rows, down_rows, is_gen)
    totals = lax.psum_scatter(stacked, "fsdp", scatter_dimension=1, tiled=True)
    share_width = totals.shape[1] // lax.axis_size("tp")
    own_slice = lax.dynamic_slice_in_dim(totals, lax.axis_index("tp") * share_width, share_width, 1)
    return (score_gap, up_grad[None], down_grad[None], own_slice[None])


def solution(mesh):
    in_specs = (
        P("fsdp", None),
        P("fsdp", None),
        P("fsdp"),
        P("group", ("fsdp", "tp"), None),
        P("group", ("fsdp", "tp"), None),
        P(),
    )
    out_specs = (
        P("fsdp", None),
        P("group", ("fsdp", "tp"), None),
        P("group", ("fsdp", "tp"), None),
        P("group", None, ("fsdp", "tp")),
    )
    return jax.shard_map(
        per_device, mesh=mesh, in_specs=in_specs, out_specs=out_specs, check_vma=False
    )
```

profile of v0, /device:TPU:0, one launch (start us, length us, event | category | flops | bytes accessed | tf_op | source)
XLA Modules:
  0.0 745.0 jit_solution(7090276212238077902)
XLA Ops:
  15.1 45.0 %all-gather.4.cloned.1.call-done = bf16[256,5120]{1,0:T(8,128)(2,1)} async-done(((bf16[32,5120]{1,0:T(8,128)(2,1)}), bf16[256,5120]{1,0:T(8,128)(2,1)}) %all-gather.4.cloned.1.call-update) | async-done | bytes 2621456 | tf_op jit(solution)/shard_map/all_gather | solution.py:62
  60.0 3.4 fusion.14
  63.4 3.2 fusion.6
  66.7 144.1 %reduce-scatter.5.cloned.1.call-done = f32[8,5120]{1,0:T(8,128)} async-done(((f32[256,5120]{1,0:T(8,128)}), f32[8,5120]{1,0:T(8,128)}) %reduce-scatter.5.cloned.1.call-update) | async-done | bytes 163856 | tf_op jit(solution)/shard_map/reduce_scatter | solution.py:37
  212.4 4.0 collective-permute-done
  217.3 8.4 %all_gather.22 = f32[32,5120]{1,0:T(8,128)S(1)} all-gather(f32[8,5120]{1,0:T(8,128)S(1)} %select_add_fusion.2), channel_id=1, replica_groups=mesh['group'=4,'fsdp'=8,'tp'=4] {'tp'}, dimensions={0}, use_global_device_ids=true | all-gather | bytes 819200 | tf_op jit(solution)/shard_map/all_gather | solution.py:46
  226.5 6.6 collective-permute-start.1
  233.2 6.6 collective-permute-done.1
  244.6 41.6 %all-gather.6.cloned.1.call-done = bf16[256,5120]{1,0:T(8,128)(2,1)} async-done(((bf16[32,5120]{1,0:T(8,128)(2,1)}), bf16[256,5120]{1,0:T(8,128)(2,1)}) %all-gather.6.cloned.1.call-update) | async-done | bytes 2621456 | tf_op jit(solution)/shard_map/all_gather | solution.py:62
  286.2 3.4 fusion.17
  293.6 144.2 %reduce-scatter.7.cloned.1.call-done = f32[8,5120]{1,0:T(8,128)} async-done(((f32[256,5120]{1,0:T(8,128)}), f32[8,5120]{1,0:T(8,128)}) %reduce-scatter.7.cloned.1.call-update) | async-done | bytes 163856 | tf_op jit(solution)/shard_map/reduce_scatter | solution.py:37
  437.7 3.8 collective-permute-start.2
  441.5 3.6 collective-permute-done.2
  446.2 8.4 %all_gather.25 = f32[32,5120]{1,0:T(8,128)S(1)} all-gather(f32[8,5120]{1,0:T(8,128)S(1)} %select_add_fusion.1), channel_id=1, replica_groups=mesh['group'=4,'fsdp'=8,'tp'=4] {'tp'}, dimensions={0}, use_global_device_ids=true | all-gather | bytes 819200 | tf_op jit(solution)/shard_map/all_gather | solution.py:46
  454.5 9.7 %all_gather.24 = f32[32,5120]{1,0:T(8,128)S(1)} all-gather(f32[8,5120]{1,0:T(8,128)} %collective-permute-done.2), channel_id=1, replica_groups=mesh['group'=4,'fsdp'=8,'tp'=4] {'tp'}, dimensions={0}, use_global_device_ids=true | all-gather | bytes 819200 | tf_op jit(solution)/shard_map/all_gather | solution.py:47
  471.0 19.4 %collective-permute-done.3 = f32[32,5120]{1,0:T(8,128)} collective-permute-done((f32[32,5120]{1,0:T(8,128)}, f32[32,5120]{1,0:T(8,128)}, u32[]{:S(2)}, u32[]{:S(2)}) %collective-permute-start.3) | collective-permute-done | bytes 655392 | tf_op jit(solution)/shard_map/ppermute | solution.py:22
  494.4 38.8 %all-gather.8.cloned.1.call-done = bf16[256,5120]{1,0:T(8,128)(2,1)} async-done(((bf16[32,5120]{1,0:T(8,128)(2,1)}), bf16[256,5120]{1,0:T(8,128)(2,1)}) %all-gather.8.cloned.1.call-update) | async-done | bytes 2621456 | tf_op jit(solution)/shard_map/all_gather | solution.py:86
  536.1 3.2 fusion.8
  539.4 143.7 %reduce-scatter.9.cloned.1.call-done = f32[8,5120]{1,0:T(8,128)} async-done(((f32[256,5120]{1,0:T(8,128)}), f32[8,5120]{1,0:T(8,128)}) %reduce-scatter.9.cloned.1.call-update) | async-done | bytes 163856 | tf_op jit(solution)/shard_map/reduce_scatter | solution.py:37
  683.1 3.8 collective-permute-start.4
  686.9 4.6 convolution_bitcast_fusion.1
  691.6 8.4 %all_gather.27 = f32[32,5120]{1,0:T(8,128)S(1)} all-gather(f32[8,5120]{1,0:T(8,128)S(1)} %select_add_fusion), channel_id=1, replica_groups=mesh['group'=4,'fsdp'=8,'tp'=4] {'tp'}, dimensions={0}, use_global_device_ids=true | all-gather | bytes 819200 | tf_op jit(solution)/shard_map/all_gather | solution.py:46
  702.8 4.9 convolution_bitcast_fusion
  707.7 29.1 %reduce-scatter.11.cloned.1.call-done = f32[5,640]{1,0:T(8,128)} async-done(((f32[5,5120]{1,0:T(8,128)}), f32[5,640]{1,0:T(8,128)}) %reduce-scatter.11.cloned.1.call-update) | async-done | bytes 12816 | tf_op jit(solution)/shard_map/reduce_scatter | solution.py:158
  (82 shorter events, 37.4 us)
Async XLA Ops:
  7.2 56.3 %copy-start = (bf16[1,216,5120]{2,1,0:T(8,128)(2,1)S(1)}, bf16[1,216,5120]{2,1,0:T(8,128)(2,1)}, u32[]{:S(2)}) copy-start(bf16[1,216,5120]{2,1,0:T(8,128)(2,1)} %param.10) | copy-start | bytes 6635524
  7.2 52.9 %all-gather.4.cloned.1.call-start = ((), (), s32[]{:S(2)}) async-start(), calls=%async_computation.4 | async-start | bytes 2949120 | tf_op jit(solution)/shard_map/all_gather | solution.py:62
  15.0 195.8 %reduce-scatter.5.cloned.1.call-start = ((), (), s32[]{:S(2)}) async-start(), calls=%async_computation.5 | async-start | bytes 5406720 | tf_op jit(solution)/shard_map/reduce_scatter | solution.py:37
  66.7 159.0 %copy-start.2 = (bf16[32,5120]{1,0:T(8,128)(2,1)S(1)}, bf16[32,5120]{1,0:T(8,128)(2,1)}, u32[]{:S(2)}) copy-start(bf16[32,5120]{1,0:T(8,128)(2,1)} %param.6) | copy-start | bytes 983044
  66.7 219.5 %all-gather.6.cloned.1.call-start = ((), (), s32[]{:S(2)}) async-start(), calls=%async_computation.6 | async-start | bytes 2949120 | tf_op jit(solution)/shard_map/all_gather | solution.py:62
  210.8 5.5 collective-permute-start
  226.5 6.7 copy-start.10
  226.5 13.3 %collective-permute-start.1 = (bf16[32,5120]{1,0:T(8,128)(2,1)S(1)}, bf16[32,5120]{1,0:T(8,128)(2,1)}, u32[]{:S(2)}, u32[]{:S(2)}) collective-permute-start(bf16[32,5120]{1,0:T(8,128)(2,1)S(1)} %fusion.46), channel_id=1, source_target_pairs={{0,64},{32,96},{1,65},{33,97},{2,66},{34,98},{3,67},{35,99},{4,68}... | collective-permute-start | bytes 983048 | tf_op jit(solution)/shard_map/ppermute | solution.py:22
  244.5 193.2 %reduce-scatter.7.cloned.1.call-start = ((), (), s32[]{:S(2)}) async-start(), calls=%async_computation.7 | async-start | bytes 5406720 | tf_op jit(solution)/shard_map/reduce_scatter | solution.py:37
  293.5 239.7 %all-gather.8.cloned.1.call-start = ((), (), s32[]{:S(2)}) async-start(), calls=%async_computation.8 | async-start | bytes 2949120 | tf_op jit(solution)/shard_map/all_gather | solution.py:86
  437.7 7.4 collective-permute-start.2
  454.5 9.7 %copy-start.3 = (f32[32,5120]{1,0:T(8,128)}, f32[32,5120]{1,0:T(8,128)S(1)}, u32[]{:S(2)}) copy-start(f32[32,5120]{1,0:T(8,128)S(1)} %all_gather.25) | copy-start | bytes 1966084
  469.6 20.7 %collective-permute-start.3 = (f32[32,5120]{1,0:T(8,128)}, f32[32,5120]{1,0:T(8,128)}, u32[]{:S(2)}, u32[]{:S(2)}) collective-permute-start(f32[32,5120]{1,0:T(8,128)} %fusion.45), channel_id=1, source_target_pairs={{64,0},{96,32},{65,1},{97,33},{66,2},{98,34},{67,3},{99,35},{68,4}... | collective-permute-start | bytes 1966088 | tf_op jit(solution)/shard_map/ppermute | solution.py:22
  470.9 22.4 %copy-start.4 = (bf16[32,5120]{1,0:T(8,128)(2,1)S(1)}, bf16[32,5120]{1,0:T(8,128)(2,1)}, u32[]{:S(2)}) copy-start(bf16[32,5120]{1,0:T(8,128)(2,1)} %get-tuple-element.18) | copy-start | bytes 983044
  470.9 22.4 %copy-start.5 = (bf16[32,5120]{1,0:T(8,128)(2,1)S(1)}, bf16[32,5120]{1,0:T(8,128)(2,1)}, u32[]{:S(2)}) copy-start(bf16[32,5120]{1,0:T(8,128)(2,1)} %get-tuple-element.14) | copy-start | bytes 983044
  470.9 22.4 %copy-start.6 = (bf16[32,5120]{1,0:T(8,128)(2,1)S(1)}, bf16[32,5120]{1,0:T(8,128)(2,1)}, u32[]{:S(2)}) copy-start(bf16[32,5120]{1,0:T(8,128)(2,1)} %get-tuple-element.15) | copy-start | bytes 983044
  470.9 22.4 %copy-start.14 = (f32[5120]{0:T(1024)S(1)}, f32[5120]{0:T(1024)}, u32[]{:S(2)}) copy-start(f32[5120]{0:T(1024)} %get-tuple-element.29) | copy-start | bytes 61444
  494.3 188.7 %reduce-scatter.9.cloned.1.call-start = ((), (), s32[]{:S(2)}) async-start(), calls=%async_computation.9 | async-start | bytes 5406720 | tf_op jit(solution)/shard_map/reduce_scatter | solution.py:37
  539.4 197.4 %reduce-scatter.11.cloned.1.call-start = ((), (), s32[]{:S(2)}) async-start(), calls=%async_computation.10 | async-start | bytes 184320 | tf_op jit(solution)/shard_map/reduce_scatter | solution.py:158
  683.1 8.5 %copy-start.13 = (f32[8,5120]{1,0:T(8,128)S(1)}, f32[8,5120]{1,0:T(8,128)}, u32[]{:S(2)}) copy-start(f32[8,5120]{1,0:T(8,128)} %reduce-scatter.9.cloned.1.call-done) | copy-start | bytes 491524
  683.1 16.9 %copy-start.12 = (f32[1,1,5120]{2,0,1:T(1,128)S(1)}, f32[1,1,5120]{2,0,1:T(1,128)}, u32[]{:S(2)}) copy-start(f32[1,1,5120]{2,0,1:T(1,128)} %copy-done.11) | copy-start | bytes 61444
  683.1 16.9 %copy-start.15 = (f32[5120]{0:T(1024)S(1)}, f32[5120]{0:T(1024)}, u32[]{:S(2)}) copy-start(f32[5120]{0:T(1024)} %get-tuple-element.28) | copy-start | bytes 61444
  683.1 16.9 %copy-start.17 = (f32[32]{0:T(128)S(1)}, f32[32]{0:T(128)}, u32[]{:S(2)}) copy-start(f32[32]{0:T(128)} %copy-done.16) | copy-start | bytes 388
  683.1 8.5 %collective-permute-start.4 = (f32[8,5120]{1,0:T(8,128)}, f32[8,5120]{1,0:T(8,128)S(1)}, u32[]{:S(2)}, u32[]{:S(2)}) collective-permute-start(f32[8,5120]{1,0:T(8,128)} %reduce-scatter.9.cloned.1.call-done), channel_id=1, source_target_pairs={{0,32},{32,0},{64,96},{96,64},{1,33},{33,1},{65,97},{97,65},{2,34}... | collective-permute-start | bytes 491528 | tf_op jit(solution)/shard_map/ppermute | solution.py:16
  (6 other events, 11.5 us)
Sparse Core Ops, SparseCore 0:
  15.1 44.8 all-gather.3
  66.8 143.9 reduce-scatter.4
  244.6 41.4 all-gather.5
  293.6 144.0 reduce-scatter.6
  494.5 38.6 all-gather.7
  539.5 143.5 reduce-scatter.8
  702.9 33.8 reduce-scatter.10
where the time goes:
time: 746 us; the launch traced here: 745 us
  waiting for transfers between devices  620 us (83%)
  blocking collectives  34.8 us (5%)
  matrix products  28.9 us (4%)
  other arithmetic  22.9 us (3%)
  starting transfers between devices  17.3 us (2%)
  between operations  15.9 us (2%)
    reduce_scatter x3, waiting for transfers between devices, hidden_total(): lax.psum_scatter(term_fn(jnp.int32(0), row_count // lax.axis_size('tp') *...  432 us
    all_gather x2, waiting for transfers between devices, forward_block(): all_rows = lax.all_gather(modulated, 'fsdp', axis=0, tiled=True)  86.6 us
    all_gather x1, waiting for transfers between devices, backward_block(): mixed_rows = lax.all_gather(mixed_grad, 'fsdp', axis=0, tiled=True)  38.8 us
    reduce_scatter x1, waiting for transfers between devices, per_device(): totals = lax.psum_scatter(stacked, 'fsdp', scatter_dimension=1, tiled=True)  29.1 us
    ppermute x2, waiting for transfers between devices, shifted(): lax.ppermute(value, axis, [(source, source + steps) for source in range(i...  25.9 us
    all_gather x3, blocking collectives, hidden_total(): lax.all_gather(shared, 'tp', axis=0, tiled=True)  25.1 us
  transfers between devices with their start and end apart: 12, of which 11 were waited for; matrix products, arithmetic and copies ran while one was open for 1% of the time, Pallas kernels for 0%

commit v1 on v0

v1 whole, which is shorter than its diff:
```python
import functools
import math

import jax
import jax.numpy as jnp
from jax import lax
from jax.experimental import pallas as pl
from jax.experimental.pallas import tpu as pltpu
from jax.sharding import PartitionSpec as P

MESH = pl.DeviceIdType.MESH
bf16, f32 = jnp.bfloat16, jnp.float32
gen_time = 999.0
epsilon_norm = 1e-06
epsilon_gap = 1e-05

D = 5120
HU = 216
HP = 256
RB = 16
PW = 1280
SW = 160
CW = 512
NT = (((1,), (1,)), ((), ()))
FAR = (1, 3, 2)


def embedding(step_value, feature_width):
    half_width = feature_width // 2
    freqs = jnp.exp(-math.log(10000.0) * jnp.arange(half_width, dtype=f32) / half_width)
    angles = step_value * freqs
    return jnp.concatenate([jnp.cos(angles), jnp.sin(angles)], axis=-1)


def device(x, y, z, c):
    return (y, lax.rem(x, 2) * 4 + z, lax.div(x, 2) * 2 + c)


def turn(value, steps):
    return lax.rem(value + (steps % 4), 4)


def gelu_parts(h):
    k = math.sqrt(2.0 / math.pi)
    t = jnp.tanh(k * (h + 0.044715 * (h * h * h)))
    value = 0.5 * h * (1.0 + t)
    slope = 0.5 * (1.0 + t) + 0.5 * h * (1.0 - t * t) * (k * (1.0 + 3.0 * 0.044715 * (h * h)))
    return value, slope


def chain_kernel(
    up_ref, down_ref, nin_ref, noi_ref, vec_ref, par_ref,
    u_out, dz_out, dht_out, at_out, score_out, small_out,
    U, W, E, G1, G2, GC, DX, uu, XH, XS, DZ, H, HS, act, DA,
    zsA, zsB, rsA, rsB, sf, ss2, r2, Z, yS, yF, X0, Dv, CS, SM, T, TR, T2, TX, T3, TZ, TY,
    loc, wss, wrs, es, er,
    a1s, a1r, a2s, a2r, b1s, b1r, b2s, b2r, c1s, c1r, c2s, c2r,
    rs1s, rs1r, rs2s, rs2r, ys, yr, xs, xr, dxs, dxr, dzs, dzr, scs, scr, sms, smr,
):
    y = lax.axis_index("group")
    fi = lax.axis_index("fsdp")
    ti = lax.axis_index("tp")
    xl, z = lax.div(fi, 4), lax.rem(fi, 4)
    xh, c = lax.div(ti, 2), lax.rem(ti, 2)
    x = xh * 2 + xl
    role = jnp.maximum(y - 1, 0)
    is_gen = y < 2
    pending = []

    def xdev(d):
        return device(turn(x, d), y, z, c)

    def zdev(d):
        return device(x, y, turn(z, d), c)

    sib = device(x, y, z, 1 - c)

    def send(src, dst, s, r, dev):
        cp = pltpu.make_async_remote_copy(
            src_ref=src, dst_ref=dst, send_sem=s, recv_sem=r, device_id=dev, device_id_type=MESH
        )
        cp.start()
        return cp

    def sent(src, s):
        pltpu.make_async_copy(src, src, s).wait()

    def arrived(dst, r):
        pltpu.make_async_copy(dst, dst, r).wait()

    loads = [
        pltpu.make_async_copy(up_ref.at[0], U.at[0], loc.at[0]),
        pltpu.make_async_copy(down_ref.at[0], W.at[0], loc.at[1]),
    ]
    for cp in loads:
        cp.start()

    barrier = pltpu.get_barrier_semaphore()
    peers = [xdev(d) for d in FAR] + [zdev(d) for d in FAR]
    peers += [device(x, turn(y, d), z, c) for d in FAR] + [sib]
    for dev in peers:
        pl.semaphore_signal(barrier, inc=1, device_id=dev, device_id_type=MESH)
    pl.semaphore_wait(barrier, len(peers))

    def own_cols(p):
        return pl.ds(pl.multiple_of(xh * (2 * PW) + p * PW, 128), PW)

    own_rows = pl.ds(pl.multiple_of(c * RB, RB), RB)

    class Gather:
        def __init__(self, buf, order, s1s, s1r, s2s, s2r):
            self.buf, self.order = buf, order
            self.sems = (s1s, s1r, s2s, s2r)

        def block(self, d1, d2):
            if self.order == "xz":
                return self.buf.at[turn(x, -d1), turn(z, -d2)]
            return self.buf.at[turn(x, -d2), turn(z, -d1)]

        def peer(self, ring, d):
            return xdev(d) if (self.order == "xz") == (ring == 1) else zdev(d)

        def first(self):
            own = self.block(0, 0)
            for d in FAR:
                send(own, own, self.sems[0].at[d - 1], self.sems[1].at[d - 1], self.peer(1, d))

        def second(self, d1):
            b = self.block(d1, 0)
            for d in FAR:
                send(b, b, self.sems[2].at[d1, d - 1], self.sems[3].at[d1, d - 1], self.peer(2, d))

        def wait1(self, d1):
            arrived(self.block(d1, 0), self.sems[1].at[d1 - 1])

        def wait2(self, d1, d2):
            arrived(self.block(d1, d2), self.sems[3].at[d1, d2 - 1])

        def drain(self):
            own = self.block(0, 0)
            for d in FAR:
                sent(own, self.sems[0].at[d - 1])
                for d1 in range(4):
                    sent(own, self.sems[2].at[d1, d - 1])

    def gather_start(A, B):
        A.first()
        B.first()
        A.second(0)
        B.second(0)

    def gather_forward(A, B):
        for d in FAR:
            A.wait1(d)
            A.second(d)
            B.wait1(d)
            B.second(d)

    def gather_group(A, B, dz):
        if dz == 0:
            for d in FAR:
                B.wait2(0, d)
        else:
            for d1 in range(4):
                A.wait2(d1, dz)
            for d in FAR:
                B.wait2(dz, d)

    g1a = Gather(G1.at[0], "xz", a1s.at[0], a1r.at[0], a2s.at[0], a2r.at[0])
    g1b = Gather(G1.at[1], "zx", b1s.at[0], b1r.at[0], b2s.at[0], b2r.at[0])
    g2a = Gather(G2.at[0], "xz", a1s.at[1], a1r.at[1], a2s.at[1], a2r.at[1])
    g2b = Gather(G2.at[1], "zx", b1s.at[1], b1r.at[1], b2s.at[1], b2r.at[1])
    g2c = Gather(GC, "xz", c1s, c1r, c2s, c2r)

    @pl.when(is_gen)
    def _():
        for p in range(2):
            G1[p, x, z] = nin_ref[own_rows, own_cols(p)]
        gather_start(g1a, g1b)

    send(up_ref.at[0], U.at[1], wss.at[0], wrs.at[0], sib)
    send(down_ref.at[0], W.at[1], wss.at[1], wrs.at[1], sib)

    @pl.when(is_gen)
    def _():
        for l in range(8):
            E[l // 4, l % 4] = vec_ref[0:1, :]

    @pl.when(jnp.logical_not(is_gen))
    def _():
        E[xl, z] = vec_ref[1:2, :]
        own = E.at[xl, z]
        for d in FAR:
            send(own, own, es.at[d - 1], er.at[d - 1], zdev(d))
        for d in FAR:
            arrived(E.at[xl, turn(z, -d)], er.at[d - 1])
        send(E.at[xl], E.at[xl], es.at[3], er.at[3], xdev(1))
        arrived(E.at[1 - xl], er.at[3])

    H[...] = jnp.zeros_like(H)
    act[...] = jnp.zeros_like(act)
    DA[...] = jnp.zeros_like(DA)

    def make_x0():
        for p in range(2):
            total = yS[0, p].astype(f32) + yS[1, p].astype(f32)
            gate = par_ref[0, 4:5, own_cols(p)] + vec_ref[0:1, own_cols(p)]
            X0[p] = (nin_ref[own_rows, own_cols(p)].astype(f32) + gate * total).astype(bf16)

    def y_send(buf, slot, k):
        for d in FAR:
            send(buf.at[slot], buf.at[slot], ys.at[k, d - 1], yr.at[k, slot], device(x, turn(y, d), z, c))

    def y_drain(buf, k):
        for d in FAR:
            sent(buf.at[0], ys.at[k, d - 1])

    @pl.when(jnp.logical_not(is_gen))
    def _():
        arrived(yS.at[0], yr.at[0, 0])
        arrived(yS.at[1], yr.at[0, 1])
        make_x0()
        for p in range(2):
            cols = own_cols(p)
            noisy = vec_ref[2:3, cols] * X0[p].astype(f32) + vec_ref[3:4, cols] * noi_ref[own_rows, cols].astype(f32)
            G1[p, x, z] = noisy.astype(bf16)
        gather_start(g1a, g1b)

    gather_forward(g1a, g1b)

    def norm_rows(zz, xl_):
        rows = pl.ds(pl.multiple_of(zz * 32 + xl_ * RB, RB), RB)

        def piece(k):
            return G1[k % 2, 2 * (k // 2) + xl_, zz].astype(f32)

        mean = sum(jnp.sum(piece(k), axis=1, keepdims=True) for k in range(4)) / D
        var = sum(jnp.sum(jnp.square(piece(k) - mean), axis=1, keepdims=True) for k in range(4)) / D
        rstd = lax.rsqrt(var + epsilon_norm)
        for k in range(4):
            cols = slice(k * PW, (k + 1) * PW)
            e = E[xl_, zz, :, cols]
            scale = 1.0 + par_ref[role, 3:4, cols] + e
            gain = (1.0 + par_ref[role, 0:1, cols]) * scale
            bias = par_ref[role, 1:2, cols] * scale + (par_ref[role, 2:3, cols] + e)
            xhat = (piece(k) - mean) * rstd
            uu[rows, cols] = (xhat * gain + bias).astype(bf16)
            XH[rows, cols] = xhat.astype(bf16)
            XS[rows, cols] = (xhat * scale).astype(bf16)

    for dz in (0, 1, 3, 2):
        gather_group(g1a, g1b, dz)
        zz = turn(z, -dz)

        def both(i, carry, zz=zz):
            norm_rows(zz, i)
            return carry

        lax.fori_loop(0, 2, both, 0)
        if dz == 0:
            for cp in loads:
                cp.wait()
            arrived(U.at[1], wrs.at[0])
        rows = pl.ds(pl.multiple_of(zz * 32, 32), 32)
        for s in range(2):
            h = lax.dot_general(uu[rows, :], U[s], NT, preferred_element_type=f32)
            H[s, rows, 0:HU] = h

    for s in range(2):
        act[s] = gelu_parts(H[s])[0].astype(bf16)
    arrived(W.at[1], wrs.at[1])

    def z_piece(xh_, p):
        cols = slice((xh_ * 2 + p) * PW, (xh_ * 2 + p + 1) * PW)
        acc = jnp.dot(act[0, :, 0:HU], W[0, :, cols], preferred_element_type=f32)
        acc += jnp.dot(act[1, :, 0:HU], W[1, :, cols], preferred_element_type=f32)
        acc = acc.astype(bf16)
        for z_ in range(4):
            for xl_ in range(2):
                rows = acc[z_ * 32 + xl_ * RB : z_ * 32 + (xl_ + 1) * RB]
                if p == 0:
                    zsA[2 * xh_ + xl_, z_] = rows
                else:
                    zsB[z_, 2 * xh_ + xl_] = rows

    z_piece(0, 0)
    z_piece(1, 0)
    for d in FAR:
        send(zsA.at[turn(x, d)], rsA.at[d - 1], rs1s.at[0, d - 1], rs1r.at[0, d - 1], xdev(d))
    z_piece(0, 1)
    z_piece(1, 1)
    for d in FAR:
        send(zsB.at[turn(z, d)], rsB.at[d - 1], rs1s.at[1, d - 1], rs1r.at[1, d - 1], zdev(d))

    half = pl.ds(0, 128)
    other = pl.ds(128, 128)
    shared = [
        (H.at[1], HS, 0),
        (uu.at[half], uu.at[other], 1),
        (XH.at[half], XH.at[other], 2),
        (XS.at[half], XS.at[other], 3),
    ]
    for src, dst, k in shared:
        send(src, dst, xs.at[k], xr.at[k], sib)

    parts = ((0, zsA, rsA, x, z, zdev), (1, zsB, rsB, z, x, xdev))
    for p, zs, rs, first, second, peer in parts:
        for d in FAR:
            arrived(rs.at[d - 1], rs1r.at[p, d - 1])

        def add(i, carry, p=p, zs=zs, rs=rs, first=first):
            total = zs[first, i].astype(f32)
            for d in range(3):
                total += rs[d, i].astype(f32)
            sf[p, i] = total
            ss2[p, i] = total.astype(bf16)
            return carry

        lax.fori_loop(0, 4, add, 0)
        for d in FAR:
            send(ss2.at[p, turn(second, d)], r2.at[p, d - 1], rs2s.at[p, d - 1], rs2r.at[p, d - 1], peer(d))
    for p, zs, rs, first, second, peer in parts:
        for d in FAR:
            arrived(r2.at[p, d - 1], rs2r.at[p, d - 1])
        total = sf[p, second]
        for d in range(3):
            total += r2[p, d].astype(f32)
        Z[p] = total

    @pl.when(is_gen)
    def _():
        for p in range(2):
            yS[y, p] = Z[p].astype(bf16)
        y_send(yS, y, 0)
        arrived(yS.at[1 - y], yr.at[0, 1 - y])
        make_x0()
        for p in range(2):
            Z[p] = yS[0, p].astype(f32) + yS[1, p].astype(f32)
        arrived(yF.at[0], yr.at[1, 0])
        arrived(yF.at[1], yr.at[1, 1])

    @pl.when(jnp.logical_not(is_gen))
    def _():
        for p in range(2):
            gate = par_ref[role, 4:5, own_cols(p)] + vec_ref[1:2, own_cols(p)]
            yF[y - 2, p] = (G1[p, x, z].astype(f32) + gate * Z[p]).astype(bf16)
        y_send(yF, y - 2, 1)
        arrived(yF.at[3 - y], yr.at[1, 3 - y])

    dist = jnp.zeros((1, 1), f32)
    for p in range(2):
        fake, real, x0 = yF[0, p].astype(f32), yF[1, p].astype(f32), X0[p].astype(f32)
        gap = (fake - real).astype(bf16)
        Dv[p] = gap
        dist += jnp.sum(jnp.sum(jnp.abs(x0 - real), axis=1, keepdims=True), axis=0, keepdims=True)
        gate = par_ref[1, 4:5, own_cols(p)] + vec_ref[1:2, own_cols(p)]
        critic = ((fake - x0) * 0.125 * gate).astype(bf16)
        G2[p, x, z] = jnp.where(y == 2, critic, gap)
    gather_start(g2a, g2b)
    CS[0] = jnp.broadcast_to(dist, (8, 128))
    cs = send(CS.at[0], CS.at[1], scs.at[0], scr.at[0], sib)

    @pl.when(y == 2)
    def _():
        for p in range(2):
            DX[xh, p] = Dv[p]
        send(DX.at[xh], DX.at[xh], dxs, dxr, xdev(2))

    cs.wait_recv()
    GC[x, z] = CS[0] + CS[1]
    g2c.first()
    g2c.second(0)
    gather_forward(g2a, g2b)
    for d in FAR:
        g2c.wait1(d)
        g2c.second(d)

    def inverse(xl_, zz):
        mean = (GC[xl_, zz] + GC[2 + xl_, zz]) / (32.0 * D)
        return 1.0 / (mean + epsilon_gap)

    def scaled_rows(zz, xl_):
        rows = pl.ds(pl.multiple_of(zz * 32 + xl_ * RB, RB), RB)
        inv = inverse(xl_, zz)[0:1, 0:1] * 0.125
        for k in range(4):
            cols = slice(k * PW, (k + 1) * PW)
            gate = par_ref[0, 4:5, cols] + vec_ref[0:1, cols]
            factor = jnp.where(y == 2, jnp.ones_like(gate), inv * gate)
            DZ[rows, cols] = (G2[k % 2, 2 * (k // 2) + xl_, zz].astype(f32) * factor).astype(bf16)

    for i, dz in enumerate((0, 1, 3, 2)):
        gather_group(g2a, g2b, dz)
        if dz > 0:
            for d1 in range(4):
                g2c.wait2(d1, dz)
        zz = turn(z, -dz)

        def both(j, carry, zz=zz):
            scaled_rows(zz, j)
            return carry

        lax.fori_loop(0, 2, both, 0)
        rows = pl.ds(pl.multiple_of(zz * 32, 32), 32)
        orows = pl.ds(pl.multiple_of(128 + zz * 32, 32), 32)
        send(DZ.at[rows], DZ.at[orows], dzs.at[i], dzr.at[i], sib)

        if dz == 0:
            inv_own = inverse(xl, z)[0:1, 0:1]

            @pl.when(y == 2)
            def _():
                arrived(DX.at[1 - xh], dxr)
                for k in range(4):
                    score_out[own_rows, k * PW : (k + 1) * PW] = DX[k // 2, k % 2].astype(f32) * inv_own

            @pl.when(y != 2)
            def _():
                for k in range(4):
                    score_out[own_rows, k * PW : (k + 1) * PW] = G2[k % 2, 2 * (k // 2) + xl, z].astype(f32) * inv_own

            send(score_out.at[own_rows], score_out.at[own_rows], scs.at[1], scr.at[1], sib)

    live = y < 3
    for s in range(2):
        rows = slice(s * 128, (s + 1) * 128)
        if s == 1:
            arrived(HS, xr.at[0])
            for i, dz in enumerate((0, 1, 3, 2)):
                orows = pl.ds(pl.multiple_of(128 + turn(z, -dz) * 32, 32), 32)
                arrived(DZ.at[orows], dzr.at[i])
        da = lax.dot_general(DZ[rows, :], W[0], NT, preferred_element_type=f32)
        DA[rows, 0:HU] = da
        value, slope = gelu_parts(H[0] if s == 0 else HS[...])
        dh = jnp.where(live, DA[rows, :] * slope, 0.0)
        DA[rows, :] = dh
        dht_out[:, rows] = dh.T.astype(bf16)
        at_out[:, rows] = jnp.where(live, value, 0.0).T.astype(bf16)

    for k in range(1, 4):
        arrived((uu, XH, XS)[k - 1].at[other], xr.at[k])
    outs = [
        pltpu.make_async_copy(uu, u_out, loc.at[2]),
        pltpu.make_async_copy(DZ, dz_out, loc.at[3]),
    ]
    for cp in outs:
        cp.start()

    latent = lax.broadcasted_iota(jnp.int32, (8, 256), 0)
    token = lax.broadcasted_iota(jnp.int32, (8, 256), 1)
    pick = (lax.div(lax.rem(token, 128), RB) == latent).astype(bf16)
    sums = jnp.dot(pick, DA[...].astype(bf16), preferred_element_type=f32)
    high = sums.astype(bf16)
    low = (sums - high.astype(f32)).astype(bf16)
    hilo = jnp.concatenate([high, low], axis=0)[:, 0:HU]
    SM[...] = jnp.zeros_like(SM)

    def small(i, carry):
        cols = pl.ds(pl.multiple_of(i * CW, CW), CW)
        uw = U[0, :, cols]
        uf = uw.astype(f32)
        both = jnp.dot(hilo, uw, preferred_element_type=f32)
        by_latent = both[0:8] + both[8:16]
        x1 = jnp.dot(dht_out[...], XH[:, cols], preferred_element_type=f32)[0:HU]
        x2 = jnp.dot(dht_out[...], XS[:, cols], preferred_element_type=f32)[0:HU]
        s1 = jnp.sum(x1 * uf, axis=0, keepdims=True)
        s2 = jnp.sum(x2 * uf, axis=0, keepdims=True)
        s3 = jnp.sum(by_latent, axis=0, keepdims=True)
        sdl = (1.0 + par_ref[role, 3:4, cols]) * s3
        for l in range(8):
            sdl += E[l % 2, l // 2, :, cols] * by_latent[l : l + 1]
        SM[0:1, cols] = s2
        SM[1:2, cols] = sdl
        SM[2:3, cols] = s3
        SM[3:4, cols] = (1.0 + par_ref[role, 0:1, cols]) * s1 + par_ref[role, 1:2, cols] * s3
        return carry

    lax.fori_loop(0, D // CW, small, 0)

    inv_own = inverse(xl, z)[0:1, 0:1]
    for p in range(2):
        fake, x0 = yF[0, p].astype(f32), X0[p].astype(f32)
        cot = jnp.where(y == 2, fake - x0, Dv[p].astype(f32) * inv_own) * 0.125
        row = jnp.sum(cot * Z[p], axis=0, keepdims=True)
        SM[4:5, own_cols(p)] = jnp.where(jnp.logical_or(y == 0, y == 2), row, 0.0)

    for k in range(32):
        start = k * SW // 128 * 128
        window = SM[:, start : start + 256]
        off = k * SW - start
        if off:
            window = pltpu.roll(window, 256 - off, 1)
        f_, t_ = k // 4, k % 4
        T[t_ % 2, (t_ // 2) * 2 + f_ // 4, f_ % 4] = window

    tc = send(T.at[1 - c], TR, sms.at[0], smr.at[0], sib)
    arrived(TR, smr.at[0])
    T2[...] = T[c] + TR[...]
    for d in FAR:
        send(T2.at[turn(x, d)], TX.at[d - 1], sms.at[d], smr.at[d], xdev(d))
    for d in FAR:
        arrived(TX.at[d - 1], smr.at[d])
    T3[...] = T2[x] + TX[0] + TX[1] + TX[2]
    for d in FAR:
        send(T3.at[turn(z, d)], TZ.at[d - 1], sms.at[3 + d], smr.at[3 + d], zdev(d))
    for d in FAR:
        arrived(TZ.at[d - 1], smr.at[3 + d])
    small_out[...] = T3[z] + TZ[0] + TZ[1] + TZ[2]

    @pl.when(is_gen)
    def _():
        TY[0] = small_out[...]
        cp = send(TY.at[0], TY.at[1], sms.at[7], smr.at[7], device(x, 1 - y, z, c))
        cp.wait()
        small_out[...] = TY[0] + TY[1]

    arrived(score_out.at[pl.ds(pl.multiple_of((1 - c) * RB, RB), RB)], scr.at[1])
    sent(score_out.at[own_rows], scs.at[1])
    sent(CS.at[0], scs.at[0])
    sent(T.at[0], sms.at[0])
    for d in FAR:
        sent(T2.at[0], sms.at[d])
        sent(T3.at[0], sms.at[3 + d])
    for g in (g1a, g1b, g2a, g2b, g2c):
        g.drain()
    sent(up_ref.at[0], wss.at[0])
    sent(down_ref.at[0], wss.at[1])
    for src, dst, k in shared:
        sent(src, xs.at[k])
    for p, zs, rs, first, second, peer in parts:
        for d in FAR:
            sent(rs.at[0], rs1s.at[p, d - 1])
            sent(r2.at[p, 0], rs2s.at[p, d - 1])
    for i in range(4):
        sent(DZ.at[pl.ds(0, 32)], dzs.at[i])

    @pl.when(is_gen)
    def _():
        y_drain(yS, 0)

    @pl.when(jnp.logical_not(is_gen))
    def _():
        y_drain(yF, 1)
        for d in FAR:
            sent(E.at[0, 0], es.at[d - 1])
        sent(E.at[0], es.at[3])

    @pl.when(y == 2)
    def _():
        sent(DX.at[0], dxs)

    for cp in outs:
        cp.wait()


def weight_kernel(dht_ref, at_ref, u_ref, dz_ref, up_ref, down_ref):
    up_ref[0] = jnp.dot(dht_ref[...], u_ref[...], preferred_element_type=f32)[0:HU]
    down_ref[0] = jnp.dot(at_ref[...], dz_ref[...], preferred_element_type=f32)[0:HU]


def per_device(noise_in, noise, timesteps, up_weight, down_weight, small_params):
    step_value = timesteps[0].astype(f32)
    angle = 0.5 * math.pi * step_value / 1000.0
    vec = jnp.stack(
        [
            embedding(jnp.float32(gen_time), D),
            embedding(step_value, D),
            jnp.full((D,), jnp.cos(angle)),
            jnp.full((D,), jnp.sin(angle)),
        ]
    )
    dma = pltpu.SemaphoreType.DMA
    vm = pltpu.VMEM
    vmem = pl.BlockSpec(memory_space=pltpu.VMEM)
    hbm = pl.BlockSpec(memory_space=pl.ANY)
    scratch = [
        vm((2, HU, D), bf16),
        vm((2, HU, D), bf16),
        vm((2, 4, 1, D), f32),
        vm((2, 4, 4, RB, PW), bf16),
        vm((2, 4, 4, RB, PW), bf16),
        vm((4, 4, 8, 128), f32),
        vm((2, 2, RB, PW), bf16),
        vm((256, D), bf16),
        vm((256, D), bf16),
        vm((256, D), bf16),
        vm((256, D), bf16),
        vm((2, 128, HP), f32),
        vm((128, HP), f32),
        vm((2, 128, HP), bf16),
        vm((256, HP), f32),
        vm((4, 4, RB, PW), bf16),
        vm((4, 4, RB, PW), bf16),
        vm((3, 4, RB, PW), bf16),
        vm((3, 4, RB, PW), bf16),
        vm((2, 4, RB, PW), f32),
        vm((2, 4, RB, PW), bf16),
        vm((2, 3, RB, PW), bf16),
        vm((2, RB, PW), f32),
        vm((2, 2, RB, PW), bf16),
        vm((2, 2, RB, PW), bf16),
        vm((2, RB, PW), bf16),
        vm((2, RB, PW), bf16),
        vm((2, 8, 128), f32),
        vm((8, D), f32),
        vm((2, 4, 4, 8, 256), f32),
        vm((4, 4, 8, 256), f32),
        vm((4, 4, 8, 256), f32),
        vm((3, 4, 8, 256), f32),
        vm((4, 8, 256), f32),
        vm((3, 8, 256), f32),
        vm((2, 8, 256), f32),
        dma((4,)), dma((2,)), dma((2,)), dma((4,)), dma((4,)),
        dma((2, 3)), dma((2, 3)), dma((2, 4, 3)), dma((2, 4, 3)),
        dma((2, 3)), dma((2, 3)), dma((2, 4, 3)), dma((2, 4, 3)),
        dma((3,)), dma((3,)), dma((4, 3)), dma((4, 3)),
        dma((2, 3)), dma((2, 3)), dma((2, 3)), dma((2, 3)),
        dma((2, 3)), dma((2, 2)), dma((4,)), dma((4,)), dma(()), dma(()),
        dma((4,)), dma((4,)), dma((2,)), dma((2,)), dma((8,)), dma((8,)),
    ]
    u_all, dz_all, dht, at, score, small = pl.pallas_call(
        chain_kernel,
        out_shape=[
            jax.ShapeDtypeStruct((256, D), bf16),
            jax.ShapeDtypeStruct((256, D), bf16),
            jax.ShapeDtypeStruct((HP, 256), bf16),
            jax.ShapeDtypeStruct((HP, 256), bf16),
            jax.ShapeDtypeStruct((32, D), f32),
            jax.ShapeDtypeStruct((8, 256), f32),
        ],
        in_specs=[hbm, hbm, vmem, vmem, vmem, vmem],
        out_specs=[hbm, hbm, vmem, vmem, vmem, vmem],
        scratch_shapes=scratch,
        compiler_params=pltpu.CompilerParams(
            collective_id=0, has_side_effects=True, vmem_limit_bytes=56 * 2**20
        ),
        name="chain",
    )(up_weight, down_weight, noise_in, noise, vec, small_params)
    full = pl.BlockSpec((HP, 256), lambda i: (0, 0))
    cols = pl.BlockSpec((256, CW), lambda i: (0, i))
    out = pl.BlockSpec((1, HU, CW), lambda i: (0, 0, i))
    up_grad, down_grad = pl.pallas_call(
        weight_kernel,
        grid=(D // CW,),
        out_shape=[jax.ShapeDtypeStruct((1, HU, D), f32)] * 2,
        in_specs=[full, full, cols, cols],
        out_specs=[out, out],
        name="weight_grads",
    )(dht, at, u_all, dz_all)
    return (score, up_grad, down_grad, small[None, 0:5, 0:SW])


def solution(mesh):
    in_specs = (
        P("fsdp", None),
        P("fsdp", None),
        P("fsdp"),
        P("group", ("fsdp", "tp"), None),
        P("group", ("fsdp", "tp"), None),
        P(),
    )
    out_specs = (
        P("fsdp", None),
        P("group", ("fsdp", "tp"), None),
        P("group", ("fsdp", "tp"), None),
        P("group", None, ("fsdp", "tp")),
    )
    return jax.shard_map(
        per_device, mesh=mesh, in_specs=in_specs, out_specs=out_specs, check_vma=False
    )
```

time: 746 us -> 128 us (0.17)
  waiting for transfers between devices: 620 us -> 0 us
  Pallas kernels: 0 us -> 121 us
  blocking collectives: 34.8 us -> 0 us
  matrix products: 28.9 us -> 0 us
  other arithmetic: 22.9 us -> 0.87 us
  starting transfers between devices: 17.3 us -> 0 us
  between operations: 15.9 us -> 1.47 us
    reduce_scatter x4 -> x0, waiting for transfers between devices: 461 us -> none  [the longest x3 432 us: hidden_total(): lax.psum_scatter(term_fn(jnp.int32(0), row_count // lax.axis_size('tp') *...]
    all_gather x3 -> x0, waiting for transfers between devices: 125 us -> none  [the longest x2 86.6 us: forward_block(): all_rows = lax.all_gather(modulated, 'fsdp', axis=0, tiled=True)]
    pallas_call x0 -> x2, Pallas kernels: none -> 121 us  [the longest x1 111 us: per_device(): pl.pallas_call(chain_kernel, out_shape=[jax.ShapeDtypeStruct((256, D), bf...]
    all_gather x4 -> x0, blocking collectives: 34.8 us -> none  [the longest x3 25.1 us: hidden_total(): lax.all_gather(shared, 'tp', axis=0, tiled=True)]
    ppermute x5 -> x0, waiting for transfers between devices: 33.5 us -> none  [the longest x2 25.9 us: shifted(): lax.ppermute(value, axis, [(source, source + steps) for source in range(i...]
    dot_general x8 -> x0, matrix products: 28.9 us -> none  [the longest x2 6.77 us: forward_block(): lax.dot_general(up_rows, all_rows, (((1,), (1,)), ((), ())), preferred_el...]
    ppermute x5 -> x0, starting transfers between devices: 17 us -> none  [the longest x3 9.16 us: partner_2(): return lax.ppermute(value, axis, pairs)]
    reduce_sum x7 -> x0, other arithmetic: 10.8 us -> none  [the longest x2 3.22 us: forward_block(): center = jnp.mean(values, axis=1, keepdims=True)]
  transfers between devices with their start and end apart: 12 -> 0, of which waited for: 11 -> 0; matrix products, arithmetic and copies ran while one was open for 1% -> 0% of each run, Pallas kernels for 0% -> 0%
where the time goes in v1:
time: 128 us
  Pallas kernels  121 us (95%)
  local copies, waits for them, and re-layouts  4.26 us (3%)
  between operations  1.47 us (1%)
    pallas_call x1, Pallas kernels, per_device(): pl.pallas_call(chain_kernel, out_shape=[jax.ShapeDtypeStruct((256, D), bf...  111 us
    pallas_call x1, Pallas kernels, per_device(): pl.pallas_call(weight_kernel, grid=(D // CW,), out_shape=[jax.ShapeDtypeS...  9.54 us
    unnamed x5, local copies, waits for them, and re-layouts  3.41 us

profile of v1, /device:TPU:0, one launch (start us, length us, event | category | flops | bytes accessed | tf_op | source)
XLA Modules:
  0.0 127.5 jit_solution(1117137107516657274)
XLA Ops:
  1.4 0.1 pad.2.clone
  1.5 0.1 pad.3.clone
  1.6 0.1 fusion.4
  1.7 0.1 fusion.2
  1.8 0.7 maximum_maximum_fusion.vec_ref
  2.5 2.0 %copy.10.par_ref = f32[3,5,5120]{2,1,0:T(8,128)} copy(f32[3,5,5120]{2,0,1:T(4,128)} %param.11) | data formatting | bytes 614400 | tf_op args[5]
  4.4 111.4 %chain.1 = (bf16[256,5120]{1,0:T(8,128)(2,1)}, bf16[256,5120]{1,0:T(8,128)(2,1)}, bf16[256,256]{1,0:T(8,128)(2,1)}, bf16[256,256]{1,0:T(8,128)(2,1)}, f32[32,5120]{1,0:T(8,128)}, /*index=5*/f32[8,256]{1,0:T(8,128)}) custom-call(bf16[1,216,5120]{2,1,0:T(8,128)(2,1)} %up_ref.1, bf16[1,216,5120]{2,1,0:T(8,128)(2,1)} %down_ref.1, bf16[32,5120]{1,0:T(8,128)(2,1)} %nin_ref.1, ...), custom_call_target="tpu_custom_call" | custom-call | tf_op jit(solution)/shard_map/chain/pallas_call | solution.py:620
  115.8 0.7 slice_bitcast_fusion
  116.5 0.6 copy.11
  117.1 0.0 copy-start
  117.1 9.5 %weight_grads.1 = (f32[1,216,5120]{2,1,0:T(8,128)}, f32[1,216,5120]{2,1,0:T(8,128)}) custom-call(bf16[256,256]{1,0:T(8,128)(2,1)} %get-tuple-element.13.dht_ref, bf16[256,256]{1,0:T(8,128)(2,1)} %get-tuple-element.14.at_ref, bf16[256,5120]{1,0:T(8,128)(2,1)} %get-tuple-element.15.u_ref, bf16[256,5120]{1,0:T(8,128)(2,1)} %get-tuple-element.16.dz_ref), custom_call_target="tpu_custom_call" | custom-call | tf_op jit(solution)/shard_map/weight_grads/pallas_call | solution.py:641
  126.7 0.0 copy-done
  126.7 0.8 copy.14
  (2 shorter events, 0.0 us)
Async XLA Ops:
  117.1 9.5 %copy-start = (f32[32,5120]{1,0:T(8,128)S(1)}, f32[32,5120]{1,0:T(8,128)}, u32[]{:S(2)}) copy-start(f32[32,5120]{1,0:T(8,128)} %get-tuple-element.32) | copy-start | bytes 1966084

commit v2 on v1

--- a/solution.py
+++ b/solution.py
@@ -24,21 +24,17 @@
 NT = (((1,), (1,)), ((), ()))
 FAR = (1, 3, 2)
 
-
 def embedding(step_value, feature_width):
     half_width = feature_width // 2
     freqs = jnp.exp(-math.log(10000.0) * jnp.arange(half_width, dtype=f32) / half_width)
     angles = step_value * freqs
     return jnp.concatenate([jnp.cos(angles), jnp.sin(angles)], axis=-1)
 
-
 def device(x, y, z, c):
     return (y, lax.rem(x, 2) * 4 + z, lax.div(x, 2) * 2 + c)
 
-
 def turn(value, steps):
     return lax.rem(value + (steps % 4), 4)
-
 
 def gelu_parts(h):
     k = math.sqrt(2.0 / math.pi)
@@ -47,15 +43,14 @@
     slope = 0.5 * (1.0 + t) + 0.5 * h * (1.0 - t * t) * (k * (1.0 + 3.0 * 0.044715 * (h * h)))
     return value, slope
 
-
 def chain_kernel(
-    up_ref, down_ref, nin_ref, noi_ref, vec_ref, par_ref,
-    u_out, dz_out, dht_out, at_out, score_out, small_out,
-    U, W, E, G1, G2, GC, DX, uu, XH, XS, DZ, H, HS, act, DA,
-    zsA, zsB, rsA, rsB, sf, ss2, r2, Z, yS, yF, X0, Dv, CS, SM, T, TR, T2, TX, T3, TZ, TY,
+    up_ref, down_ref, nin_ref, noi_ref, vec_ref, par_hbm,
+    uu, DZ, dht_out, at_out, score_out, small_out,
+    par_ref, U, UT, W, E, G1, G2, GC, DX, XH, H, HS, act, DA, dhb,
+    zsA, zsB, rsA, rsB, sf, ss2, r2, Z, yS, yF, X0, Dv, CS, SM, T, TX, T3, TZ,
     loc, wss, wrs, es, er,
     a1s, a1r, a2s, a2r, b1s, b1r, b2s, b2r, c1s, c1r, c2s, c2r,
-    rs1s, rs1r, rs2s, rs2r, ys, yr, xs, xr, dxs, dxr, dzs, dzr, scs, scr, sms, smr,
+    rsAs, rsAr, rsBs, rsBr, rs2s, rs2r, ys, yr, xs, xr, dxs, dxr, dzs, dzr, scs, scr, t1s, t1r, t2s, t2r,
 ):
     y = lax.axis_index("group")
     fi = lax.axis_index("fsdp")
@@ -89,8 +84,9 @@
         pltpu.make_async_copy(dst, dst, r).wait()
 
     loads = [
-        pltpu.make_async_copy(up_ref.at[0], U.at[0], loc.at[0]),
+        pltpu.make_async_copy(up_ref.at[0], U, loc.at[0]),
         pltpu.make_async_copy(down_ref.at[0], W.at[0], loc.at[1]),
+        pltpu.make_async_copy(par_hbm, par_ref, loc.at[2]),
     ]
     for cp in loads:
         cp.start()
@@ -98,6 +94,9 @@
     barrier = pltpu.get_barrier_semaphore()
     peers = [xdev(d) for d in FAR] + [zdev(d) for d in FAR]
     peers += [device(x, turn(y, d), z, c) for d in FAR] + [sib]
+    twin = y + 1 - 2 * lax.rem(y, 2)
+    peers += [device(turn(x, d), y, z, 1 - c) for d in FAR]
+    peers += [device(x, twin, turn(z, d), c) for d in FAR]
     for dev in peers:
         pl.semaphore_signal(barrier, inc=1, device_id=dev, device_id_type=MESH)
     pl.semaphore_wait(barrier, len(peers))
@@ -178,8 +177,17 @@
             G1[p, x, z] = nin_ref[own_rows, own_cols(p)]
         gather_start(g1a, g1b)
 
-    send(up_ref.at[0], U.at[1], wss.at[0], wrs.at[0], sib)
+    loads[0].wait()
+
+    def transpose(i, carry):
+        cols = pl.ds(pl.multiple_of(i * CW, CW), CW)
+        UT[0, cols, :] = U[:, cols].T
+        return carry
+
+    lax.fori_loop(0, D // CW, transpose, 0)
+    send(UT.at[0], UT.at[1], wss.at[0], wrs.at[0], sib)
     send(down_ref.at[0], W.at[1], wss.at[1], wrs.at[1], sib)
+    loads[2].wait()
 
     @pl.when(is_gen)
     def _():
@@ -201,30 +209,36 @@
     act[...] = jnp.zeros_like(act)
     DA[...] = jnp.zeros_like(DA)
 
-    def make_x0():
+    def make_x0(p):
+        total = yS[0, p].astype(f32) + yS[1, p].astype(f32)
+        gate = par_ref[0, 4:5, own_cols(p)] + vec_ref[0:1, own_cols(p)]
+        X0[p] = (nin_ref[own_rows, own_cols(p)].astype(f32) + gate * total).astype(bf16)
+
+    def y_send(buf, slot, p, k):
+        own = buf.at[slot, p]
+        for d in FAR:
+            send(own, own, ys.at[k, p, d - 1], yr.at[k, p, slot], device(x, turn(y, d), z, c))
+
+    def y_wait(buf, slot, p, k):
+        arrived(buf.at[slot, p], yr.at[k, p, slot])
+
+    def y_drain(buf, k):
         for p in range(2):
-            total = yS[0, p].astype(f32) + yS[1, p].astype(f32)
-            gate = par_ref[0, 4:5, own_cols(p)] + vec_ref[0:1, own_cols(p)]
-            X0[p] = (nin_ref[own_rows, own_cols(p)].astype(f32) + gate * total).astype(bf16)
-
-    def y_send(buf, slot, k):
-        for d in FAR:
-            send(buf.at[slot], buf.at[slot], ys.at[k, d - 1], yr.at[k, slot], device(x, turn(y, d), z, c))
-
-    def y_drain(buf, k):
-        for d in FAR:
-            sent(buf.at[0], ys.at[k, d - 1])
+            for d in FAR:
+                sent(buf.at[0, 0], ys.at[k, p, d - 1])
 
     @pl.when(jnp.logical_not(is_gen))
     def _():
-        arrived(yS.at[0], yr.at[0, 0])
-        arrived(yS.at[1], yr.at[0, 1])
-        make_x0()
-        for p in range(2):
+        for p, g in ((0, g1a), (1, g1b)):
+            y_wait(yS, 0, p, 0)
+            y_wait(yS, 1, p, 0)
+            make_x0(p)
             cols = own_cols(p)
             noisy = vec_ref[2:3, cols] * X0[p].astype(f32) + vec_ref[3:4, cols] * noi_ref[own_rows, cols].astype(f32)
             G1[p, x, z] = noisy.astype(bf16)
-        gather_start(g1a, g1b)
+            g.first()
+        g1a.second(0)
+        g1b.second(0)
 
     gather_forward(g1a, g1b)
 
@@ -246,7 +260,6 @@
             xhat = (piece(k) - mean) * rstd
             uu[rows, cols] = (xhat * gain + bias).astype(bf16)
             XH[rows, cols] = xhat.astype(bf16)
-            XS[rows, cols] = (xhat * scale).astype(bf16)
 
     for dz in (0, 1, 3, 2):
         gather_group(g1a, g1b, dz)
@@ -257,17 +270,14 @@
             return carry
 
         lax.fori_loop(0, 2, both, 0)
-        if dz == 0:
-            for cp in loads:
-                cp.wait()
-            arrived(U.at[1], wrs.at[0])
-        rows = pl.ds(pl.multiple_of(zz * 32, 32), 32)
-        for s in range(2):
-            h = lax.dot_general(uu[rows, :], U[s], NT, preferred_element_type=f32)
-            H[s, rows, 0:HU] = h
+
+    arrived(UT.at[1], wrs.at[0])
+    for s in range(2):
+        H[s, :, 0:HU] = jnp.dot(uu[0:128, :], UT[s], preferred_element_type=f32)
 
     for s in range(2):
         act[s] = gelu_parts(H[s])[0].astype(bf16)
+    loads[1].wait()
     arrived(W.at[1], wrs.at[1])
 
     def z_piece(xh_, p):
@@ -283,14 +293,23 @@
                 else:
                     zsB[z_, 2 * xh_ + xl_] = rows
 
-    z_piece(0, 0)
-    z_piece(1, 0)
-    for d in FAR:
-        send(zsA.at[turn(x, d)], rsA.at[d - 1], rs1s.at[0, d - 1], rs1r.at[0, d - 1], xdev(d))
-    z_piece(0, 1)
-    z_piece(1, 1)
-    for d in FAR:
-        send(zsB.at[turn(z, d)], rsB.at[d - 1], rs1s.at[1, d - 1], rs1r.at[1, d - 1], zdev(d))
+    for xh_ in range(2):
+        z_piece(xh_, 0)
+        for xl_ in range(2):
+            to = 2 * xh_ + xl_
+
+            @pl.when(to != x)
+            def _():
+                d = lax.rem(to + 4 - x, 4)
+                send(zsA.at[to], rsA.at[d - 1], rsAs.at[d - 1], rsAr.at[d - 1], device(to, y, z, c))
+
+        z_piece(xh_, 1)
+        two = pl.ds(2 * xh_, 2)
+        for d in FAR:
+            send(
+                zsB.at[turn(z, d), two], rsB.at[d - 1, two],
+                rsBs.at[d - 1, xh_], rsBr.at[d - 1, xh_], zdev(d),
+            )
 
     half = pl.ds(0, 128)
     other = pl.ds(128, 128)
@@ -298,7 +317,6 @@
         (H.at[1], HS, 0),
         (uu.at[half], uu.at[other], 1),
         (XH.at[half], XH.at[other], 2),
-        (XS.at[half], XS.at[other], 3),
     ]
     for src, dst, k in shared:
         send(src, dst, xs.at[k], xr.at[k], sib)
@@ -306,7 +324,11 @@
     parts = ((0, zsA, rsA, x, z, zdev), (1, zsB, rsB, z, x, xdev))
     for p, zs, rs, first, second, peer in parts:
         for d in FAR:
-            arrived(rs.at[d - 1], rs1r.at[p, d - 1])
+            if p == 0:
+                arrived(rsA.at[d - 1], rsAr.at[d - 1])
+            else:
+                for xh_ in range(2):
+                    arrived(rsB.at[d - 1, pl.ds(2 * xh_, 2)], rsBr.at[d - 1, xh_])
 
         def add(i, carry, p=p, zs=zs, rs=rs, first=first):
             total = zs[first, i].astype(f32)
@@ -327,28 +349,35 @@
             total += r2[p, d].astype(f32)
         Z[p] = total
 
+        @pl.when(is_gen)
+        def _(p=p, total=total):
+            yS[y, p] = total.astype(bf16)
+            y_send(yS, y, p, 0)
+
+        @pl.when(jnp.logical_not(is_gen))
+        def _(p=p, total=total):
+            gate = par_ref[role, 4:5, own_cols(p)] + vec_ref[1:2, own_cols(p)]
+            yF[y - 2, p] = (G1[p, x, z].astype(f32) + gate * total).astype(bf16)
+            y_send(yF, y - 2, p, 1)
+
     @pl.when(is_gen)
     def _():
         for p in range(2):
-            yS[y, p] = Z[p].astype(bf16)
-        y_send(yS, y, 0)
-        arrived(yS.at[1 - y], yr.at[0, 1 - y])
-        make_x0()
-        for p in range(2):
+            y_wait(yS, 1 - y, p, 0)
+            make_x0(p)
             Z[p] = yS[0, p].astype(f32) + yS[1, p].astype(f32)
-        arrived(yF.at[0], yr.at[1, 0])
-        arrived(yF.at[1], yr.at[1, 1])
-
-    @pl.when(jnp.logical_not(is_gen))
-    def _():
-        for p in range(2):
-            gate = par_ref[role, 4:5, own_cols(p)] + vec_ref[1:2, own_cols(p)]
-            yF[y - 2, p] = (G1[p, x, z].astype(f32) + gate * Z[p]).astype(bf16)
-        y_send(yF, y - 2, 1)
-        arrived(yF.at[3 - y], yr.at[1, 3 - y])
 
     dist = jnp.zeros((1, 1), f32)
-    for p in range(2):
+    for p, g in ((0, g2a), (1, g2b)):
+        @pl.when(is_gen)
+        def _(p=p):
+            y_wait(yF, 0, p, 1)
+            y_wait(yF, 1, p, 1)
+
+        @pl.when(jnp.logical_not(is_gen))
+        def _(p=p):
+            y_wait(yF, 3 - y, p, 1)
+
         fake, real, x0 = yF[0, p].astype(f32), yF[1, p].astype(f32), X0[p].astype(f32)
         gap = (fake - real).astype(bf16)
         Dv[p] = gap
@@ -356,7 +385,9 @@
         gate = par_ref[1, 4:5, own_cols(p)] + vec_ref[1:2, own_cols(p)]
         critic = ((fake - x0) * 0.125 * gate).astype(bf16)
         G2[p, x, z] = jnp.where(y == 2, critic, gap)
-    gather_start(g2a, g2b)
+        g.first()
+    g2a.second(0)
+    g2b.second(0)
     CS[0] = jnp.broadcast_to(dist, (8, 128))
     cs = send(CS.at[0], CS.at[1], scs.at[0], scr.at[0], sib)
 
@@ -421,57 +452,41 @@
             send(score_out.at[own_rows], score_out.at[own_rows], scs.at[1], scr.at[1], sib)
 
     live = y < 3
+    arrived(HS, xr.at[0])
+    for i, dz in enumerate((0, 1, 3, 2)):
+        orows = pl.ds(pl.multiple_of(128 + turn(z, -dz) * 32, 32), 32)
+        arrived(DZ.at[orows], dzr.at[i])
+    DA[:, 0:HU] = lax.dot_general(DZ[...], W[0], NT, preferred_element_type=f32)
     for s in range(2):
         rows = slice(s * 128, (s + 1) * 128)
-        if s == 1:
-            arrived(HS, xr.at[0])
-            for i, dz in enumerate((0, 1, 3, 2)):
-                orows = pl.ds(pl.multiple_of(128 + turn(z, -dz) * 32, 32), 32)
-                arrived(DZ.at[orows], dzr.at[i])
-        da = lax.dot_general(DZ[rows, :], W[0], NT, preferred_element_type=f32)
-        DA[rows, 0:HU] = da
         value, slope = gelu_parts(H[0] if s == 0 else HS[...])
         dh = jnp.where(live, DA[rows, :] * slope, 0.0)
-        DA[rows, :] = dh
+        dhb[rows, :] = dh.astype(bf16)
         dht_out[:, rows] = dh.T.astype(bf16)
         at_out[:, rows] = jnp.where(live, value, 0.0).T.astype(bf16)
 
-    for k in range(1, 4):
-        arrived((uu, XH, XS)[k - 1].at[other], xr.at[k])
-    outs = [
-        pltpu.make_async_copy(uu, u_out, loc.at[2]),
-        pltpu.make_async_copy(DZ, dz_out, loc.at[3]),
-    ]
-    for cp in outs:
-        cp.start()
-
-    latent = lax.broadcasted_iota(jnp.int32, (8, 256), 0)
-    token = lax.broadcasted_iota(jnp.int32, (8, 256), 1)
-    pick = (lax.div(lax.rem(token, 128), RB) == latent).astype(bf16)
-    sums = jnp.dot(pick, DA[...].astype(bf16), preferred_element_type=f32)
-    high = sums.astype(bf16)
-    low = (sums - high.astype(f32)).astype(bf16)
-    hilo = jnp.concatenate([high, low], axis=0)[:, 0:HU]
+    for k in range(1, 3):
+        arrived((uu, XH)[k - 1].at[other], xr.at[k])
+
     SM[...] = jnp.zeros_like(SM)
 
     def small(i, carry):
         cols = pl.ds(pl.multiple_of(i * CW, CW), CW)
-        uw = U[0, :, cols]
-        uf = uw.astype(f32)
-        both = jnp.dot(hilo, uw, preferred_element_type=f32)
-        by_latent = both[0:8] + both[8:16]
-        x1 = jnp.dot(dht_out[...], XH[:, cols], preferred_element_type=f32)[0:HU]
-        x2 = jnp.dot(dht_out[...], XS[:, cols], preferred_element_type=f32)[0:HU]
-        s1 = jnp.sum(x1 * uf, axis=0, keepdims=True)
-        s2 = jnp.sum(x2 * uf, axis=0, keepdims=True)
-        s3 = jnp.sum(by_latent, axis=0, keepdims=True)
-        sdl = (1.0 + par_ref[role, 3:4, cols]) * s3
+        du = jnp.dot(dhb[:, 0:HU], U[:, cols], preferred_element_type=f32)
+        dx = du * XH[:, cols].astype(f32)
+        p3 = 1.0 + par_ref[role, 3:4, cols]
+        rows = [jnp.zeros((1, CW), f32) for _ in range(4)]
         for l in range(8):
-            sdl += E[l % 2, l // 2, :, cols] * by_latent[l : l + 1]
-        SM[0:1, cols] = s2
-        SM[1:2, cols] = sdl
-        SM[2:3, cols] = s3
-        SM[3:4, cols] = (1.0 + par_ref[role, 0:1, cols]) * s1 + par_ref[role, 1:2, cols] * s3
+            first, second = slice(l * RB, (l + 1) * RB), slice(128 + l * RB, 128 + (l + 1) * RB)
+            plain = jnp.sum(du[first] + du[second], axis=0, keepdims=True)
+            norm = jnp.sum(dx[first] + dx[second], axis=0, keepdims=True)
+            scale = p3 + E[l % 2, l // 2, :, cols]
+            for k, term in enumerate((scale * norm, scale * plain, plain, norm)):
+                rows[k] += term
+        SM[0:1, cols] = rows[0]
+        SM[1:2, cols] = rows[1]
+        SM[2:3, cols] = rows[2]
+        SM[3:4, cols] = (1.0 + par_ref[role, 0:1, cols]) * rows[3] + par_ref[role, 1:2, cols] * rows[2]
         return carry
 
     lax.fori_loop(0, D // CW, small, 0)
@@ -492,43 +507,53 @@
         f_, t_ = k // 4, k % 4
         T[t_ % 2, (t_ // 2) * 2 + f_ // 4, f_ % 4] = window
 
-    tc = send(T.at[1 - c], TR, sms.at[0], smr.at[0], sib)
-    arrived(TR, smr.at[0])
-    T2[...] = T[c] + TR[...]
-    for d in FAR:
-        send(T2.at[turn(x, d)], TX.at[d - 1], sms.at[d], smr.at[d], xdev(d))
-    for d in FAR:
-        arrived(TX.at[d - 1], smr.at[d])
-    T3[...] = T2[x] + TX[0] + TX[1] + TX[2]
-    for d in FAR:
-        send(T3.at[turn(z, d)], TZ.at[d - 1], sms.at[3 + d], smr.at[3 + d], zdev(d))
-    for d in FAR:
-        arrived(TZ.at[d - 1], smr.at[3 + d])
+    near = [(dx, dc) for dc in range(2) for dx in (0, 1, 3, 2) if dx + dc]
+    for k, (dx, dc) in enumerate(near):
+        c_ = c if dc == 0 else 1 - c
+        send(T.at[c_, turn(x, dx)], TX.at[k], t1s.at[k], t1r.at[k], device(turn(x, dx), y, z, c_))
+    for k in range(7):
+        arrived(TX.at[k], t1r.at[k])
+    T3[...] = T[c, x] + ((TX[0] + TX[1] + TX[2]) + (TX[3] + TX[4] + TX[5] + TX[6]))
+    for k, d in enumerate(FAR):
+        send(T3.at[turn(z, d)], TZ.at[k], t2s.at[k], t2r.at[k], zdev(d))
+
+    @pl.when(is_gen)
+    def _():
+        for k in range(4):
+            d = (0,) + FAR
+            send(T3.at[turn(z, d[k])], TZ.at[3 + k], t2s.at[3 + k], t2r.at[3 + k], device(x, twin, turn(z, d[k]), c))
+
+    for k in range(3):
+        arrived(TZ.at[k], t2r.at[k])
     small_out[...] = T3[z] + TZ[0] + TZ[1] + TZ[2]
 
     @pl.when(is_gen)
     def _():
-        TY[0] = small_out[...]
-        cp = send(TY.at[0], TY.at[1], sms.at[7], smr.at[7], device(x, 1 - y, z, c))
-        cp.wait()
-        small_out[...] = TY[0] + TY[1]
+        for k in range(4):
+            arrived(TZ.at[3 + k], t2r.at[3 + k])
+            sent(TZ.at[3 + k], t2s.at[3 + k])
+        small_out[...] = small_out[...] + (TZ[3] + TZ[4] + TZ[5] + TZ[6])
 
     arrived(score_out.at[pl.ds(pl.multiple_of((1 - c) * RB, RB), RB)], scr.at[1])
     sent(score_out.at[own_rows], scs.at[1])
     sent(CS.at[0], scs.at[0])
-    sent(T.at[0], sms.at[0])
-    for d in FAR:
-        sent(T2.at[0], sms.at[d])
-        sent(T3.at[0], sms.at[3 + d])
+    for k in range(7):
+        sent(TX.at[k], t1s.at[k])
+    for k in range(3):
+        sent(TZ.at[k], t2s.at[k])
     for g in (g1a, g1b, g2a, g2b, g2c):
         g.drain()
-    sent(up_ref.at[0], wss.at[0])
+    sent(UT.at[0], wss.at[0])
     sent(down_ref.at[0], wss.at[1])
     for src, dst, k in shared:
         sent(src, xs.at[k])
     for p, zs, rs, first, second, peer in parts:
         for d in FAR:
-            sent(rs.at[0], rs1s.at[p, d - 1])
+            if p == 0:
+                sent(rs.at[0], rsAs.at[d - 1])
+            else:
+                for xh_ in range(2):
+                    sent(rs.at[0, pl.ds(0, 2)], rsBs.at[d - 1, xh_])
             sent(r2.at[p, 0], rs2s.at[p, d - 1])
     for i in range(4):
         sent(DZ.at[pl.ds(0, 32)], dzs.at[i])
@@ -548,14 +573,40 @@
     def _():
         sent(DX.at[0], dxs)
 
-    for cp in outs:
-        cp.wait()
-
-
-def weight_kernel(dht_ref, at_ref, u_ref, dz_ref, up_ref, down_ref):
-    up_ref[0] = jnp.dot(dht_ref[...], u_ref[...], preferred_element_type=f32)[0:HU]
-    down_ref[0] = jnp.dot(at_ref[...], dz_ref[...], preferred_element_type=f32)[0:HU]
-
+def weight_kernel(dht_ref, at_ref, u_ref, dz_ref, up_ref, down_ref, ubuf, dbuf, usem, dsem):
+    count = D // CW
+
+    def copies(i, slot):
+        cols = pl.ds(pl.multiple_of(i * CW, CW), CW)
+        return (
+            pltpu.make_async_copy(ubuf.at[slot], up_ref.at[0, :, cols], usem.at[slot]),
+            pltpu.make_async_copy(dbuf.at[slot], down_ref.at[0, :, cols], dsem.at[slot]),
+        )
+
+    def step(i, carry):
+        slot = lax.rem(i, 2)
+        cols = pl.ds(pl.multiple_of(i * CW, CW), CW)
+        up_copy, down_copy = copies(i, slot)
+
+        @pl.when(i >= 2)
+        def _():
+            up_copy.wait()
+
+        ubuf[slot] = jnp.dot(dht_ref[...], u_ref[:, cols], preferred_element_type=f32)[0:HU]
+        up_copy.start()
+
+        @pl.when(i >= 2)
+        def _():
+            down_copy.wait()
+
+        dbuf[slot] = jnp.dot(at_ref[...], dz_ref[:, cols], preferred_element_type=f32)[0:HU]
+        down_copy.start()
+        return carry
+
+    lax.fori_loop(0, count, step, 0)
+    for i in (count - 2, count - 1):
+        for cp in copies(i, i % 2):
+            cp.wait()
 
 def per_device(noise_in, noise, timesteps, up_weight, down_weight, small_params):
     step_value = timesteps[0].astype(f32)
@@ -573,7 +624,9 @@
     vmem = pl.BlockSpec(memory_space=pltpu.VMEM)
     hbm = pl.BlockSpec(memory_space=pl.ANY)
     scratch = [
-        vm((2, HU, D), bf16),
+        vm((3, 5, D), f32),
+        vm((HU, D), bf16),
+        vm((2, D, HU), bf16),
         vm((2, HU, D), bf16),
         vm((2, 4, 1, D), f32),
         vm((2, 4, 4, RB, PW), bf16),
@@ -581,13 +634,11 @@
         vm((4, 4, 8, 128), f32),
         vm((2, 2, RB, PW), bf16),
         vm((256, D), bf16),
-        vm((256, D), bf16),
-        vm((256, D), bf16),
-        vm((256, D), bf16),
         vm((2, 128, HP), f32),
         vm((128, HP), f32),
         vm((2, 128, HP), bf16),
         vm((256, HP), f32),
+        vm((256, HP), bf16),
         vm((4, 4, RB, PW), bf16),
         vm((4, 4, RB, PW), bf16),
         vm((3, 4, RB, PW), bf16),
@@ -603,51 +654,45 @@
         vm((2, 8, 128), f32),
         vm((8, D), f32),
         vm((2, 4, 4, 8, 256), f32),
-        vm((4, 4, 8, 256), f32),
-        vm((4, 4, 8, 256), f32),
-        vm((3, 4, 8, 256), f32),
+        vm((7, 4, 8, 256), f32),
         vm((4, 8, 256), f32),
-        vm((3, 8, 256), f32),
-        vm((2, 8, 256), f32),
-        dma((4,)), dma((2,)), dma((2,)), dma((4,)), dma((4,)),
+        vm((7, 8, 256), f32),
+        dma((3,)), dma((2,)), dma((2,)), dma((4,)), dma((4,)),
         dma((2, 3)), dma((2, 3)), dma((2, 4, 3)), dma((2, 4, 3)),
         dma((2, 3)), dma((2, 3)), dma((2, 4, 3)), dma((2, 4, 3)),
         dma((3,)), dma((3,)), dma((4, 3)), dma((4, 3)),
-        dma((2, 3)), dma((2, 3)), dma((2, 3)), dma((2, 3)),
-        dma((2, 3)), dma((2, 2)), dma((4,)), dma((4,)), dma(()), dma(()),
-        dma((4,)), dma((4,)), dma((2,)), dma((2,)), dma((8,)), dma((8,)),
+        dma((3,)), dma((3,)), dma((3, 2)), dma((3, 2)), dma((2, 3)), dma((2, 3)),
+        dma((2, 2, 3)), dma((2, 2, 2)), dma((3,)), dma((3,)), dma(()), dma(()),
+        dma((4,)), dma((4,)), dma((2,)), dma((2,)), dma((7,)), dma((7,)), dma((7,)), dma((7,)),
     ]
     u_all, dz_all, dht, at, score, small = pl.pallas_call(
         chain_kernel,
         out_shape=[
-            jax.ShapeDtypeStruct((256, D), bf16),
-            jax.ShapeDtypeStruct((256, D), bf16),
-            jax.ShapeDtypeStruct((HP, 256), bf16),
-            jax.ShapeDtypeStruct((HP, 256), bf16),
+            vm((256, D), bf16),
+            vm((256, D), bf16),
+            vm((HP, 256), bf16),
+            vm((HP, 256), bf16),
             jax.ShapeDtypeStruct((32, D), f32),
             jax.ShapeDtypeStruct((8, 256), f32),
         ],
-        in_specs=[hbm, hbm, vmem, vmem, vmem, vmem],
-        out_specs=[hbm, hbm, vmem, vmem, vmem, vmem],
+        in_specs=[hbm, hbm, vmem, vmem, vmem, hbm],
+        out_specs=[vmem] * 6,
         scratch_shapes=scratch,
         compiler_params=pltpu.CompilerParams(
-            collective_id=0, has_side_effects=True, vmem_limit_bytes=56 * 2**20
+            collective_id=0, has_side_effects=True, vmem_limit_bytes=52 * 2**20
         ),
         name="chain",
     )(up_weight, down_weight, noise_in, noise, vec, small_params)
-    full = pl.BlockSpec((HP, 256), lambda i: (0, 0))
-    cols = pl.BlockSpec((256, CW), lambda i: (0, i))
-    out = pl.BlockSpec((1, HU, CW), lambda i: (0, 0, i))
     up_grad, down_grad = pl.pallas_call(
         weight_kernel,
-        grid=(D // CW,),
         out_shape=[jax.ShapeDtypeStruct((1, HU, D), f32)] * 2,
-        in_specs=[full, full, cols, cols],
-        out_specs=[out, out],
+        in_specs=[vmem] * 4,
+        out_specs=[hbm, hbm],
+        scratch_shapes=[vm((2, HU, CW), f32), vm((2, HU, CW), f32), dma((2,)), dma((2,))],
+        compiler_params=pltpu.CompilerParams(vmem_limit_bytes=24 * 2**20),
         name="weight_grads",
     )(dht, at, u_all, dz_all)
     return (score, up_grad, down_grad, small[None, 0:5, 0:SW])
-
 
 def solution(mesh):
     in_specs = (

time: 128 us -> 111 us (0.87)
  Pallas kernels: 121 us -> 105 us
    pallas_call x2, Pallas kernels: 121 us -> 105 us  [the longest x1 98.9 us: per_device(): pl.pallas_call(chain_kernel, out_shape=[vm((256, D), bf16), vm((256, D),...]
where the time goes in v2:
time: 111 us
  Pallas kernels  105 us (95%)
  local copies, waits for them, and re-layouts  4.26 us (4%)
  between operations  1.49 us (1%)
    pallas_call x1, Pallas kernels, per_device(): pl.pallas_call(chain_kernel, out_shape=[vm((256, D), bf16), vm((256, D),...  98.9 us
    pallas_call x1, Pallas kernels, per_device(): pl.pallas_call(weight_kernel, out_shape=[jax.ShapeDtypeStruct((1, HU, D),...  5.64 us
    unnamed x5, local copies, waits for them, and re-layouts  3.41 us

profile of v2, /device:TPU:0, one launch (start us, length us, event | category | flops | bytes accessed | tf_op | source)
XLA Modules:
  0.0 111.2 jit_solution(6091621231027292868)
XLA Ops:
  1.4 0.1 pad.2.clone
  1.5 0.1 pad.3.clone
  1.6 0.1 fusion.4
  1.7 0.1 fusion.2
  1.8 0.7 maximum_maximum_fusion.vec_ref
  2.5 2.0 %copy.10.par_hbm = f32[3,5,5120]{2,1,0:T(8,128)} copy(f32[3,5,5120]{2,0,1:T(4,128)} %param.11) | data formatting | bytes 614400 | tf_op args[5]
  4.4 98.9 %chain.1 = (bf16[256,5120]{1,0:T(8,128)(2,1)S(1)}, bf16[256,5120]{1,0:T(8,128)(2,1)S(1)}, bf16[256,256]{1,0:T(8,128)(2,1)S(1)}, bf16[256,256]{1,0:T(8,128)(2,1)S...) custom-call(bf16[1,216,5120]{2,1,0:T(8,128)(2,1)} %up_ref.1, bf16[1,216,5120]{2,1,0:T(8,128)(2,1)} %down_ref.1, ...), custom_call_target="tpu_custom_call" | custom-call | tf_op jit(solution)/shard_map/chain/pallas_call | solution.py:668
  103.4 0.7 slice_bitcast_fusion
  104.1 0.6 copy.11
  104.7 0.0 copy-start
  104.7 5.6 %weight_grads.1 = (f32[1,216,5120]{2,1,0:T(8,128)}, f32[1,216,5120]{2,1,0:T(8,128)}) custom-call(bf16[256,256]{1,0:T(8,128)(2,1)S(1)} %get-tuple-element.13.dht_ref, bf16[256,256]{1,0:T(8,128)(2,1)S(1)} %get-tuple-element.14.at_ref, bf16[256,5120]{1,0:T(8,128)(2,1)S(1)} %get-tuple-element.15.u_ref, bf16[256,5120]{1,0:T(8,128)(2,1)S(1)} %get-tuple-element.16.dz_ref), custom_call_target="tpu_custom_call" | custom-call | tf_op jit(solution)/shard_map/weight_grads/pallas_call | solution.py:686
  110.3 0.0 copy-done
  110.3 0.8 copy.14
  (2 shorter events, 0.0 us)
Async XLA Ops:
  104.7 5.7 %copy-start = (f32[32,5120]{1,0:T(8,128)S(1)}, f32[32,5120]{1,0:T(8,128)}, u32[]{:S(2)}) copy-start(f32[32,5120]{1,0:T(8,128)} %get-tuple-element.32) | copy-start | bytes 1966084

commit v3 on v2

--- a/solution.py
+++ b/solution.py
@@ -45,11 +45,11 @@
 
 def chain_kernel(
     up_ref, down_ref, nin_ref, noi_ref, vec_ref, par_hbm,
-    uu, DZ, dht_out, at_out, score_out, small_out,
-    par_ref, U, UT, W, E, G1, G2, GC, DX, XH, H, HS, act, DA, dhb,
-    zsA, zsB, rsA, rsB, sf, ss2, r2, Z, yS, yF, X0, Dv, CS, SM, T, TX, T3, TZ,
+    GU, GD, score_out, small_out,
+    uu, DZ, par_ref, PR, dht, at, IV, U, UT, W, E, G1, G2A, G2B, DX, XH, H, HS, act, DA, dhb,
+    zsA, zsB, rsA, rsB, sf, ss2, r2, Z, yS, yF, X0, Dv, CS, SM, T, T16, TX, T3, TZ,
     loc, wss, wrs, es, er,
-    a1s, a1r, a2s, a2r, b1s, b1r, b2s, b2r, c1s, c1r, c2s, c2r,
+    a1s, a1r, a2s, a2r, b1s, b1r, b2s, b2r,
     rsAs, rsAr, rsBs, rsBr, rs2s, rs2r, ys, yr, xs, xr, dxs, dxr, dzs, dzr, scs, scr, t1s, t1r, t2s, t2r,
 ):
     y = lax.axis_index("group")
@@ -167,9 +167,8 @@
 
     g1a = Gather(G1.at[0], "xz", a1s.at[0], a1r.at[0], a2s.at[0], a2r.at[0])
     g1b = Gather(G1.at[1], "zx", b1s.at[0], b1r.at[0], b2s.at[0], b2r.at[0])
-    g2a = Gather(G2.at[0], "xz", a1s.at[1], a1r.at[1], a2s.at[1], a2r.at[1])
-    g2b = Gather(G2.at[1], "zx", b1s.at[1], b1r.at[1], b2s.at[1], b2r.at[1])
-    g2c = Gather(GC, "xz", c1s, c1r, c2s, c2r)
+    g2a = Gather(G2A, "xz", a1s.at[1], a1r.at[1], a2s.at[1], a2r.at[1])
+    g2b = Gather(G2B, "zx", b1s.at[1], b1r.at[1], b2s.at[1], b2r.at[1])
 
     @pl.when(is_gen)
     def _():
@@ -188,6 +187,10 @@
     send(UT.at[0], UT.at[1], wss.at[0], wrs.at[0], sib)
     send(down_ref.at[0], W.at[1], wss.at[1], wrs.at[1], sib)
     loads[2].wait()
+    for j in range(5):
+        PR[j : j + 1, :] = par_ref[j, pl.ds(role, 1), :]
+    PR[5:6, :] = par_ref[4, 0:1, :]
+    PR[6:7, :] = par_ref[4, 1:2, :]
 
     @pl.when(is_gen)
     def _():
@@ -211,7 +214,7 @@
 
     def make_x0(p):
         total = yS[0, p].astype(f32) + yS[1, p].astype(f32)
-        gate = par_ref[0, 4:5, own_cols(p)] + vec_ref[0:1, own_cols(p)]
+        gate = PR[5:6, own_cols(p)] + vec_ref[0:1, own_cols(p)]
         X0[p] = (nin_ref[own_rows, own_cols(p)].astype(f32) + gate * total).astype(bf16)
 
     def y_send(buf, slot, p, k):
@@ -254,9 +257,9 @@
         for k in range(4):
             cols = slice(k * PW, (k + 1) * PW)
             e = E[xl_, zz, :, cols]
-            scale = 1.0 + par_ref[role, 3:4, cols] + e
-            gain = (1.0 + par_ref[role, 0:1, cols]) * scale
-            bias = par_ref[role, 1:2, cols] * scale + (par_ref[role, 2:3, cols] + e)
+            scale = 1.0 + PR[3:4, cols] + e
+            gain = (1.0 + PR[0:1, cols]) * scale
+            bias = PR[1:2, cols] * scale + (PR[2:3, cols] + e)
             xhat = (piece(k) - mean) * rstd
             uu[rows, cols] = (xhat * gain + bias).astype(bf16)
             XH[rows, cols] = xhat.astype(bf16)
@@ -356,7 +359,7 @@
 
         @pl.when(jnp.logical_not(is_gen))
         def _(p=p, total=total):
-            gate = par_ref[role, 4:5, own_cols(p)] + vec_ref[1:2, own_cols(p)]
+            gate = PR[4:5, own_cols(p)] + vec_ref[1:2, own_cols(p)]
             yF[y - 2, p] = (G1[p, x, z].astype(f32) + gate * total).astype(bf16)
             y_send(yF, y - 2, p, 1)
 
@@ -381,15 +384,24 @@
         fake, real, x0 = yF[0, p].astype(f32), yF[1, p].astype(f32), X0[p].astype(f32)
         gap = (fake - real).astype(bf16)
         Dv[p] = gap
-        dist += jnp.sum(jnp.sum(jnp.abs(x0 - real), axis=1, keepdims=True), axis=0, keepdims=True)
-        gate = par_ref[1, 4:5, own_cols(p)] + vec_ref[1:2, own_cols(p)]
+        dist += jnp.sum(jnp.sum(jnp.abs(x0 - real), axis=0, keepdims=True), axis=1, keepdims=True)
+        gate = PR[6:7, own_cols(p)] + vec_ref[1:2, own_cols(p)]
         critic = ((fake - x0) * 0.125 * gate).astype(bf16)
-        G2[p, x, z] = jnp.where(y == 2, critic, gap)
-        g.first()
+        block = jnp.where(y == 2, critic, gap)
+        if p == 0:
+            G2A[x, z, :, 0:PW] = block
+        else:
+            G2B[x, z] = block
+    hi = dist.astype(bf16)
+    mid = (dist - hi.astype(f32)).astype(bf16)
+    low = (dist - hi.astype(f32) - mid.astype(f32)).astype(bf16)
+    lane = lax.broadcasted_iota(jnp.int32, (RB, 128), 1)
+    tile = jnp.where(lane == 0, hi.astype(f32), jnp.where(lane == 1, mid.astype(f32), low.astype(f32)))
+    G2A[x, z, :, PW:] = tile.astype(bf16)
+    g2a.first()
+    g2b.first()
     g2a.second(0)
     g2b.second(0)
-    CS[0] = jnp.broadcast_to(dist, (8, 128))
-    cs = send(CS.at[0], CS.at[1], scs.at[0], scr.at[0], sib)
 
     @pl.when(y == 2)
     def _():
@@ -397,33 +409,32 @@
             DX[xh, p] = Dv[p]
         send(DX.at[xh], DX.at[xh], dxs, dxr, xdev(2))
 
-    cs.wait_recv()
-    GC[x, z] = CS[0] + CS[1]
-    g2c.first()
-    g2c.second(0)
     gather_forward(g2a, g2b)
-    for d in FAR:
-        g2c.wait1(d)
-        g2c.second(d)
-
-    def inverse(xl_, zz):
-        mean = (GC[xl_, zz] + GC[2 + xl_, zz]) / (32.0 * D)
-        return 1.0 / (mean + epsilon_gap)
+
+    def gap_piece(k, xl_, zz):
+        col = 2 * (k // 2) + xl_
+        return G2A[col, zz, :, 0:PW] if k % 2 == 0 else G2B[col, zz]
+
+    def share(xl_, zz):
+        def one(col):
+            tile = G2A[col, zz, :, PW:].astype(f32)
+            return (tile[0:1, 0:1] + tile[0:1, 1:2]) + tile[0:1, 2:3]
+
+        return one(xl_) + one(2 + xl_)
+
+    def inverse(l):
+        return 1.0 / ((CS[0, l : l + 1, :] + CS[1, l : l + 1, :]) / (32.0 * D) + epsilon_gap)
 
     def scaled_rows(zz, xl_):
         rows = pl.ds(pl.multiple_of(zz * 32 + xl_ * RB, RB), RB)
-        inv = inverse(xl_, zz)[0:1, 0:1] * 0.125
         for k in range(4):
             cols = slice(k * PW, (k + 1) * PW)
-            gate = par_ref[0, 4:5, cols] + vec_ref[0:1, cols]
-            factor = jnp.where(y == 2, jnp.ones_like(gate), inv * gate)
-            DZ[rows, cols] = (G2[k % 2, 2 * (k // 2) + xl_, zz].astype(f32) * factor).astype(bf16)
+            gate = PR[5:6, cols] + vec_ref[0:1, cols]
+            factor = jnp.where(y == 2, jnp.ones_like(gate), gate * 0.125)
+            DZ[rows, cols] = (gap_piece(k, xl_, zz).astype(f32) * factor).astype(bf16)
 
     for i, dz in enumerate((0, 1, 3, 2)):
         gather_group(g2a, g2b, dz)
-        if dz > 0:
-            for d1 in range(4):
-                g2c.wait2(d1, dz)
         zz = turn(z, -dz)
 
         def both(j, carry, zz=zz):
@@ -435,38 +446,27 @@
         orows = pl.ds(pl.multiple_of(128 + zz * 32, 32), 32)
         send(DZ.at[rows], DZ.at[orows], dzs.at[i], dzr.at[i], sib)
 
-        if dz == 0:
-            inv_own = inverse(xl, z)[0:1, 0:1]
-
-            @pl.when(y == 2)
-            def _():
-                arrived(DX.at[1 - xh], dxr)
-                for k in range(4):
-                    score_out[own_rows, k * PW : (k + 1) * PW] = DX[k // 2, k % 2].astype(f32) * inv_own
-
-            @pl.when(y != 2)
-            def _():
-                for k in range(4):
-                    score_out[own_rows, k * PW : (k + 1) * PW] = G2[k % 2, 2 * (k // 2) + xl, z].astype(f32) * inv_own
-
-            send(score_out.at[own_rows], score_out.at[own_rows], scs.at[1], scr.at[1], sib)
-
+    for l in range(8):
+        CS[0, l : l + 1, :] = jnp.broadcast_to(share(l % 2, l // 2), (1, 128))
+    send(CS.at[0], CS.at[1], scs.at[0], scr.at[0], sib)
     live = y < 3
     arrived(HS, xr.at[0])
     for i, dz in enumerate((0, 1, 3, 2)):
         orows = pl.ds(pl.multiple_of(128 + turn(z, -dz) * 32, 32), 32)
         arrived(DZ.at[orows], dzr.at[i])
     DA[:, 0:HU] = lax.dot_general(DZ[...], W[0], NT, preferred_element_type=f32)
+    arrived(CS.at[1], scr.at[0])
+    for l in range(8):
+        inv = jnp.where(y == 2, 1.0, inverse(l)[:, 0:1])
+        IV[l * RB : (l + 1) * RB, :] = jnp.broadcast_to(inv, (RB, 256))
     for s in range(2):
         rows = slice(s * 128, (s + 1) * 128)
         value, slope = gelu_parts(H[0] if s == 0 else HS[...])
-        dh = jnp.where(live, DA[rows, :] * slope, 0.0)
+        dh = jnp.where(live, DA[rows, :] * slope * IV[...], 0.0)
+        DA[rows, :] = dh
         dhb[rows, :] = dh.astype(bf16)
-        dht_out[:, rows] = dh.T.astype(bf16)
-        at_out[:, rows] = jnp.where(live, value, 0.0).T.astype(bf16)
-
-    for k in range(1, 3):
-        arrived((uu, XH)[k - 1].at[other], xr.at[k])
+
+    arrived(XH.at[other], xr.at[2])
 
     SM[...] = jnp.zeros_like(SM)
 
@@ -474,24 +474,42 @@
         cols = pl.ds(pl.multiple_of(i * CW, CW), CW)
         du = jnp.dot(dhb[:, 0:HU], U[:, cols], preferred_element_type=f32)
         dx = du * XH[:, cols].astype(f32)
-        p3 = 1.0 + par_ref[role, 3:4, cols]
-        rows = [jnp.zeros((1, CW), f32) for _ in range(4)]
+        p3 = 1.0 + PR[3:4, cols]
+        rows = [jnp.zeros((8, CW), f32) for _ in range(4)]
         for l in range(8):
-            first, second = slice(l * RB, (l + 1) * RB), slice(128 + l * RB, 128 + (l + 1) * RB)
-            plain = jnp.sum(du[first] + du[second], axis=0, keepdims=True)
-            norm = jnp.sum(dx[first] + dx[second], axis=0, keepdims=True)
+            starts = [l * RB + k for k in (0, 8, 128, 136)]
+            plain = sum(du[k : k + 8] for k in starts)
+            norm = sum(dx[k : k + 8] for k in starts)
             scale = p3 + E[l % 2, l // 2, :, cols]
             for k, term in enumerate((scale * norm, scale * plain, plain, norm)):
                 rows[k] += term
+        rows = [jnp.sum(row, axis=0, keepdims=True) for row in rows]
         SM[0:1, cols] = rows[0]
         SM[1:2, cols] = rows[1]
         SM[2:3, cols] = rows[2]
-        SM[3:4, cols] = (1.0 + par_ref[role, 0:1, cols]) * rows[3] + par_ref[role, 1:2, cols] * rows[2]
+        SM[3:4, cols] = (1.0 + PR[0:1, cols]) * rows[3] + PR[1:2, cols] * rows[2]
         return carry
 
     lax.fori_loop(0, D // CW, small, 0)
 
-    inv_own = inverse(xl, z)[0:1, 0:1]
+    own_row = pl.ds(z * 2 + xl, 1)
+    inv_own = (1.0 / ((CS[0, own_row, :] + CS[1, own_row, :]) / (32.0 * D) + epsilon_gap))[:, 0:1]
+
+    @pl.when(y == 2)
+    def _():
+        arrived(DX.at[1 - xh], dxr)
+        for k in range(4):
+            score_out[own_rows, k * PW : (k + 1) * PW] = DX[k // 2, k % 2].astype(f32) * inv_own
+
+    @pl.when(y != 2)
+    def _():
+        for k in range(4):
+            score_out[own_rows, k * PW : (k + 1) * PW] = gap_piece(k, xl, z).astype(f32) * inv_own
+
+    send(score_out.at[own_rows], score_out.at[own_rows], scs.at[1], scr.at[1], sib)
+
+    own_row = pl.ds(z * 2 + xl, 1)
+    inv_own = (1.0 / ((CS[0, own_row, :] + CS[1, own_row, :]) / (32.0 * D) + epsilon_gap))[:, 0:1]
     for p in range(2):
         fake, x0 = yF[0, p].astype(f32), X0[p].astype(f32)
         cot = jnp.where(y == 2, fake - x0, Dv[p].astype(f32) * inv_own) * 0.125
@@ -505,15 +523,39 @@
         if off:
             window = pltpu.roll(window, 256 - off, 1)
         f_, t_ = k // 4, k % 4
-        T[t_ % 2, (t_ // 2) * 2 + f_ // 4, f_ % 4] = window
-
+        row = f_ % 4 * 8
+        T[t_ % 2, (t_ // 2) * 2 + f_ // 4, row : row + 8] = window
+
+    T16[...] = T[...].astype(bf16)
     near = [(dx, dc) for dc in range(2) for dx in (0, 1, 3, 2) if dx + dc]
     for k, (dx, dc) in enumerate(near):
         c_ = c if dc == 0 else 1 - c
-        send(T.at[c_, turn(x, dx)], TX.at[k], t1s.at[k], t1r.at[k], device(turn(x, dx), y, z, c_))
+        send(T16.at[c_, turn(x, dx)], TX.at[k], t1s.at[k], t1r.at[k], device(turn(x, dx), y, z, c_))
+
+    live_rows = jnp.where(live, IV[...], 0.0)
+    for s in range(2):
+        rows = slice(s * 128, (s + 1) * 128)
+        value = gelu_parts(H[0] if s == 0 else HS[...])[0]
+        dht[:, rows] = DA[rows, :].T.astype(bf16)
+        at[:, rows] = (value * live_rows).T.astype(bf16)
+    arrived(uu.at[other], xr.at[1])
+
+    def product(left, right, out):
+        def step(i, carry):
+            cols = pl.ds(pl.multiple_of(i * CW, CW), CW)
+            out[:, cols] = jnp.dot(left[...], right[:, cols], preferred_element_type=f32)[0:HU]
+            return carry
+
+        lax.fori_loop(0, D // CW, step, 0)
+
+    product(dht, uu, GU)
     for k in range(7):
         arrived(TX.at[k], t1r.at[k])
-    T3[...] = T[c, x] + ((TX[0] + TX[1] + TX[2]) + (TX[3] + TX[4] + TX[5] + TX[6]))
+    total = T[c, x]
+    for k in range(7):
+        total += TX[k].astype(f32)
+    for z_ in range(4):
+        T3[z_] = total[z_ * 8 : z_ * 8 + 8]
     for k, d in enumerate(FAR):
         send(T3.at[turn(z, d)], TZ.at[k], t2s.at[k], t2r.at[k], zdev(d))
 
@@ -522,6 +564,8 @@
         for k in range(4):
             d = (0,) + FAR
             send(T3.at[turn(z, d[k])], TZ.at[3 + k], t2s.at[3 + k], t2r.at[3 + k], device(x, twin, turn(z, d[k]), c))
+
+    product(at, DZ, GD)
 
     for k in range(3):
         arrived(TZ.at[k], t2r.at[k])
@@ -541,7 +585,7 @@
         sent(TX.at[k], t1s.at[k])
     for k in range(3):
         sent(TZ.at[k], t2s.at[k])
-    for g in (g1a, g1b, g2a, g2b, g2c):
+    for g in (g1a, g1b, g2a, g2b):
         g.drain()
     sent(UT.at[0], wss.at[0])
     sent(down_ref.at[0], wss.at[1])
@@ -573,40 +617,19 @@
     def _():
         sent(DX.at[0], dxs)
 
-def weight_kernel(dht_ref, at_ref, u_ref, dz_ref, up_ref, down_ref, ubuf, dbuf, usem, dsem):
-    count = D // CW
-
-    def copies(i, slot):
-        cols = pl.ds(pl.multiple_of(i * CW, CW), CW)
-        return (
-            pltpu.make_async_copy(ubuf.at[slot], up_ref.at[0, :, cols], usem.at[slot]),
-            pltpu.make_async_copy(dbuf.at[slot], down_ref.at[0, :, cols], dsem.at[slot]),
-        )
-
-    def step(i, carry):
-        slot = lax.rem(i, 2)
-        cols = pl.ds(pl.multiple_of(i * CW, CW), CW)
-        up_copy, down_copy = copies(i, slot)
-
-        @pl.when(i >= 2)
-        def _():
-            up_copy.wait()
-
-        ubuf[slot] = jnp.dot(dht_ref[...], u_ref[:, cols], preferred_element_type=f32)[0:HU]
-        up_copy.start()
-
-        @pl.when(i >= 2)
-        def _():
-            down_copy.wait()
-
-        dbuf[slot] = jnp.dot(at_ref[...], dz_ref[:, cols], preferred_element_type=f32)[0:HU]
-        down_copy.start()
-        return carry
-
-    lax.fori_loop(0, count, step, 0)
-    for i in (count - 2, count - 1):
-        for cp in copies(i, i % 2):
-            cp.wait()
+def place_kernel(gu, gd, score, small, up_out, down_out, score_out, small_out, sems):
+    cuts = ((0, 56), (56, 56), (112, 56), (168, 48))
+    copies = [pltpu.make_async_copy(score, score_out, sems.at[0])]
+    for k, (start, size) in enumerate(cuts):
+        rows = pl.ds(start, size)
+        copies.append(pltpu.make_async_copy(gu.at[rows], up_out.at[0, rows], sems.at[1 + k]))
+        copies.append(pltpu.make_async_copy(gd.at[rows], down_out.at[0, rows], sems.at[5 + k]))
+    for cp in copies:
+        cp.start()
+    for k in range(5):
+        small_out[k] = small[k : k + 1, 0:SW]
+    for cp in copies:
+        cp.wait()
 
 def per_device(noise_in, noise, timesteps, up_weight, down_weight, small_params):
     step_value = timesteps[0].astype(f32)
@@ -624,14 +647,20 @@
     vmem = pl.BlockSpec(memory_space=pltpu.VMEM)
     hbm = pl.BlockSpec(memory_space=pl.ANY)
     scratch = [
-        vm((3, 5, D), f32),
+        vm((256, D), bf16),
+        vm((256, D), bf16),
+        vm((5, 3, D), f32),
+        vm((8, D), f32),
+        vm((HP, 256), bf16),
+        vm((HP, 256), bf16),
+        vm((128, 256), f32),
         vm((HU, D), bf16),
         vm((2, D, HU), bf16),
         vm((2, HU, D), bf16),
         vm((2, 4, 1, D), f32),
         vm((2, 4, 4, RB, PW), bf16),
-        vm((2, 4, 4, RB, PW), bf16),
-        vm((4, 4, 8, 128), f32),
+        vm((4, 4, RB, PW + 128), bf16),
+        vm((4, 4, RB, PW), bf16),
         vm((2, 2, RB, PW), bf16),
         vm((256, D), bf16),
         vm((2, 128, HP), f32),
@@ -653,46 +682,49 @@
         vm((2, RB, PW), bf16),
         vm((2, 8, 128), f32),
         vm((8, D), f32),
-        vm((2, 4, 4, 8, 256), f32),
-        vm((7, 4, 8, 256), f32),
+        vm((2, 4, 32, 256), f32),
+        vm((2, 4, 32, 256), bf16),
+        vm((7, 32, 256), bf16),
         vm((4, 8, 256), f32),
         vm((7, 8, 256), f32),
         dma((3,)), dma((2,)), dma((2,)), dma((4,)), dma((4,)),
         dma((2, 3)), dma((2, 3)), dma((2, 4, 3)), dma((2, 4, 3)),
         dma((2, 3)), dma((2, 3)), dma((2, 4, 3)), dma((2, 4, 3)),
-        dma((3,)), dma((3,)), dma((4, 3)), dma((4, 3)),
         dma((3,)), dma((3,)), dma((3, 2)), dma((3, 2)), dma((2, 3)), dma((2, 3)),
         dma((2, 2, 3)), dma((2, 2, 2)), dma((3,)), dma((3,)), dma(()), dma(()),
         dma((4,)), dma((4,)), dma((2,)), dma((2,)), dma((7,)), dma((7,)), dma((7,)), dma((7,)),
     ]
-    u_all, dz_all, dht, at, score, small = pl.pallas_call(
+    parts = pl.pallas_call(
         chain_kernel,
         out_shape=[
-            vm((256, D), bf16),
-            vm((256, D), bf16),
-            vm((HP, 256), bf16),
-            vm((HP, 256), bf16),
-            jax.ShapeDtypeStruct((32, D), f32),
-            jax.ShapeDtypeStruct((8, 256), f32),
+            vm((HU, D), f32),
+            vm((HU, D), f32),
+            vm((32, D), f32),
+            vm((8, 256), f32),
         ],
         in_specs=[hbm, hbm, vmem, vmem, vmem, hbm],
-        out_specs=[vmem] * 6,
+        out_specs=[vmem] * 4,
         scratch_shapes=scratch,
         compiler_params=pltpu.CompilerParams(
             collective_id=0, has_side_effects=True, vmem_limit_bytes=52 * 2**20
         ),
         name="chain",
-    )(up_weight, down_weight, noise_in, noise, vec, small_params)
-    up_grad, down_grad = pl.pallas_call(
-        weight_kernel,
-        out_shape=[jax.ShapeDtypeStruct((1, HU, D), f32)] * 2,
+    )(up_weight, down_weight, noise_in, noise, vec, jnp.transpose(small_params, (1, 0, 2)))
+    up_grad, down_grad, score, small = pl.pallas_call(
+        place_kernel,
+        out_shape=[
+            jax.ShapeDtypeStruct((1, HU, D), f32),
+            jax.ShapeDtypeStruct((1, HU, D), f32),
+            jax.ShapeDtypeStruct((32, D), f32),
+            jax.ShapeDtypeStruct((5, 1, SW), f32),
+        ],
         in_specs=[vmem] * 4,
-        out_specs=[hbm, hbm],
-        scratch_shapes=[vm((2, HU, CW), f32), vm((2, HU, CW), f32), dma((2,)), dma((2,))],
+        out_specs=[hbm, hbm, hbm, vmem],
+        scratch_shapes=[dma((9,))],
         compiler_params=pltpu.CompilerParams(vmem_limit_bytes=24 * 2**20),
-        name="weight_grads",
-    )(dht, at, u_all, dz_all)
-    return (score, up_grad, down_grad, small[None, 0:5, 0:SW])
+        name="place",
+    )(*parts)
+    return (score, up_grad, down_grad, jnp.transpose(small, (1, 0, 2)))
 
 def solution(mesh):
     in_specs = (

time: 111 us -> 103 us (0.928)
  Pallas kernels: 105 us -> 100 us
  local copies, waits for them, and re-layouts: 4.26 us -> 0.15 us
    pallas_call x2, Pallas kernels: 105 us -> 100 us  [the longest x1 95.8 us: per_device(): pl.pallas_call(chain_kernel, out_shape=[vm((HU, D), f32), vm((HU, D), f32...]
    unnamed x5 -> x0, local copies, waits for them, and re-layouts: 3.41 us -> none
where the time goes in v3:
time: 103 us
  Pallas kernels  100 us (97%)
  between operations  1.47 us (1%)
    pallas_call x1, Pallas kernels, per_device(): pl.pallas_call(chain_kernel, out_shape=[vm((HU, D), f32), vm((HU, D), f32...  95.8 us
    pallas_call x1, Pallas kernels, per_device(): pl.pallas_call(place_kernel, out_shape=[jax.ShapeDtypeStruct((1, HU, D),...  4.33 us

profile of v3, /device:TPU:0, one launch (start us, length us, event | category | flops | bytes accessed | tf_op | source)
XLA Modules:
  0.0 102.6 jit_solution(6831428918403851713)
XLA Ops:
  1.4 0.1 pad.2.clone
  1.5 0.1 pad.3.clone
  1.6 0.1 fusion.4
  1.7 0.1 fusion.2
  1.8 0.7 maximum_maximum_fusion.vec_ref
  2.5 95.8 %chain.1 = (f32[216,5120]{1,0:T(8,128)S(1)}, f32[216,5120]{1,0:T(8,128)S(1)}, f32[32,5120]{1,0:T(8,128)S(1)}, f32[8,256]{1,0:T(8,128)S(1)}) custom-call(bf16[1,216,5120]{2,1,0:T(8,128)(2,1)} %up_ref.1, bf16[1,216,5120]{2,1,0:T(8,128)(2,1)} %down_ref.1, bf16[32,5120]{1,0:T(8,128)(2,1)} %nin_ref.1, bf16[32,5120]{1,0:T(8,128)(2,1)} %noi_ref.1, ...), custom_call_target="tpu_custom_call" | custom-call | tf_op jit(solution)/shard_map/chain/pallas_call | solution.py:697
  98.3 4.3 %place.1 = (f32[1,216,5120]{2,1,0:T(8,128)}, f32[1,216,5120]{2,1,0:T(8,128)}, f32[32,5120]{1,0:T(8,128)}, f32[5,1,160]{2,1,0:T(1,128)}) custom-call(f32[216,5120]{1,0:T(8,128)S(1)} %get-tuple-element.12.gu, f32[216,5120]{1,0:T(8,128)S(1)} %get-tuple-element.13.gd, f32[32,5120]{1,0:T(8,128)S(1)} %get-tuple-element.14.score, f32[8,256]{1,0:T(8,128)S(1)} %get-tuple-element.15.small), custom_call_target="tpu_custom_call" | custom-call | tf_op jit(solution)/shard_map/place/pallas_call | solution.py:713
  (2 shorter events, 0.0 us)

commit v4 on v3

--- a/solution.py
+++ b/solution.py
@@ -20,9 +20,9 @@
 RB = 16
 PW = 1280
 SW = 160
-CW = 512
+CW = 1024
 NT = (((1,), (1,)), ((), ()))
-FAR = (1, 3, 2)
+FAR = (2, 1, 3)
 
 def embedding(step_value, feature_width):
     half_width = feature_width // 2
@@ -44,9 +44,9 @@
     return value, slope
 
 def chain_kernel(
-    up_ref, down_ref, nin_ref, noi_ref, vec_ref, par_hbm,
-    GU, GD, score_out, small_out,
-    uu, DZ, par_ref, PR, dht, at, IV, U, UT, W, E, G1, G2A, G2B, DX, XH, H, HS, act, DA, dhb,
+    up_ref, down_ref, nin_hbm, noi_hbm, vec_ref, par_hbm,
+    GU, at, DZ, score_out, small_out,
+    nin_ref, noi_ref, uu, par_ref, PR, dht, IV, U, UT, W, E, G1, G2A, G2B, DX, XH, H, HS, act, DA, dhb,
     zsA, zsB, rsA, rsB, sf, ss2, r2, Z, yS, yF, X0, Dv, CS, SM, T, T16, TX, T3, TZ,
     loc, wss, wrs, es, er,
     a1s, a1r, a2s, a2r, b1s, b1r, b2s, b2r,
@@ -83,12 +83,16 @@
     def arrived(dst, r):
         pltpu.make_async_copy(dst, dst, r).wait()
 
+    early = [
+        pltpu.make_async_copy(nin_hbm, nin_ref, loc.at[3]),
+        pltpu.make_async_copy(noi_hbm, noi_ref, loc.at[4]),
+    ]
     loads = [
         pltpu.make_async_copy(up_ref.at[0], U, loc.at[0]),
         pltpu.make_async_copy(down_ref.at[0], W.at[0], loc.at[1]),
         pltpu.make_async_copy(par_hbm, par_ref, loc.at[2]),
     ]
-    for cp in loads:
+    for cp in early + loads:
         cp.start()
 
     barrier = pltpu.get_barrier_semaphore()
@@ -100,6 +104,8 @@
     for dev in peers:
         pl.semaphore_signal(barrier, inc=1, device_id=dev, device_id_type=MESH)
     pl.semaphore_wait(barrier, len(peers))
+    for cp in early:
+        cp.wait()
 
     def own_cols(p):
         return pl.ds(pl.multiple_of(xh * (2 * PW) + p * PW, 128), PW)
@@ -219,8 +225,8 @@
 
     def y_send(buf, slot, p, k):
         own = buf.at[slot, p]
-        for d in FAR:
-            send(own, own, ys.at[k, p, d - 1], yr.at[k, p, slot], device(x, turn(y, d), z, c))
+        for i, to in enumerate((3 - y, turn(y, 2), twin)):
+            send(own, own, ys.at[k, p, i], yr.at[k, p, slot], device(x, to, z, c))
 
     def y_wait(buf, slot, p, k):
         arrived(buf.at[slot, p], yr.at[k, p, slot])
@@ -565,8 +571,6 @@
             d = (0,) + FAR
             send(T3.at[turn(z, d[k])], TZ.at[3 + k], t2s.at[3 + k], t2r.at[3 + k], device(x, twin, turn(z, d[k]), c))
 
-    product(at, DZ, GD)
-
     for k in range(3):
         arrived(TZ.at[k], t2r.at[k])
     small_out[...] = T3[z] + TZ[0] + TZ[1] + TZ[2]
@@ -617,17 +621,22 @@
     def _():
         sent(DX.at[0], dxs)
 
-def place_kernel(gu, gd, score, small, up_out, down_out, score_out, small_out, sems):
+def place_kernel(gu, at, dz, score, small, up_out, down_out, score_out, small_out, gd, sems, down_sems):
     cuts = ((0, 56), (56, 56), (112, 56), (168, 48))
     copies = [pltpu.make_async_copy(score, score_out, sems.at[0])]
     for k, (start, size) in enumerate(cuts):
         rows = pl.ds(start, size)
         copies.append(pltpu.make_async_copy(gu.at[rows], up_out.at[0, rows], sems.at[1 + k]))
-        copies.append(pltpu.make_async_copy(gd.at[rows], down_out.at[0, rows], sems.at[5 + k]))
     for cp in copies:
         cp.start()
     for k in range(5):
         small_out[k] = small[k : k + 1, 0:SW]
+    for i in range(D // CW):
+        cols = pl.ds(i * CW, CW)
+        gd[:, cols] = jnp.dot(at[...], dz[:, cols], preferred_element_type=f32)[0:HU]
+        cp = pltpu.make_async_copy(gd.at[:, cols], down_out.at[0, :, cols], down_sems.at[i])
+        cp.start()
+        copies.append(cp)
     for cp in copies:
         cp.wait()
 
@@ -647,11 +656,11 @@
     vmem = pl.BlockSpec(memory_space=pltpu.VMEM)
     hbm = pl.BlockSpec(memory_space=pl.ANY)
     scratch = [
-        vm((256, D), bf16),
+        vm((32, D), bf16),
+        vm((32, D), bf16),
         vm((256, D), bf16),
         vm((5, 3, D), f32),
         vm((8, D), f32),
-        vm((HP, 256), bf16),
         vm((HP, 256), bf16),
         vm((128, 256), f32),
         vm((HU, D), bf16),
@@ -687,7 +696,7 @@
         vm((7, 32, 256), bf16),
         vm((4, 8, 256), f32),
         vm((7, 8, 256), f32),
-        dma((3,)), dma((2,)), dma((2,)), dma((4,)), dma((4,)),
+        dma((5,)), dma((2,)), dma((2,)), dma((4,)), dma((4,)),
         dma((2, 3)), dma((2, 3)), dma((2, 4, 3)), dma((2, 4, 3)),
         dma((2, 3)), dma((2, 3)), dma((2, 4, 3)), dma((2, 4, 3)),
         dma((3,)), dma((3,)), dma((3, 2)), dma((3, 2)), dma((2, 3)), dma((2, 3)),
@@ -698,12 +707,13 @@
         chain_kernel,
         out_shape=[
             vm((HU, D), f32),
-            vm((HU, D), f32),
+            vm((HP, 256), bf16),
+            vm((256, D), bf16),
             vm((32, D), f32),
             vm((8, 256), f32),
         ],
-        in_specs=[hbm, hbm, vmem, vmem, vmem, hbm],
-        out_specs=[vmem] * 4,
+        in_specs=[hbm, hbm, hbm, hbm, vmem, hbm],
+        out_specs=[vmem] * 5,
         scratch_shapes=scratch,
         compiler_params=pltpu.CompilerParams(
             collective_id=0, has_side_effects=True, vmem_limit_bytes=52 * 2**20
@@ -718,9 +728,9 @@
             jax.ShapeDtypeStruct((32, D), f32),
             jax.ShapeDtypeStruct((5, 1, SW), f32),
         ],
-        in_specs=[vmem] * 4,
+        in_specs=[vmem] * 5,
         out_specs=[hbm, hbm, hbm, vmem],
-        scratch_shapes=[dma((9,))],
+        scratch_shapes=[vm((HU, D), f32), dma((5,)), dma((D // CW,))],
         compiler_params=pltpu.CompilerParams(vmem_limit_bytes=24 * 2**20),
         name="place",
     )(*parts)

time: 103 us -> 100 us (0.971)
  Pallas kernels: 100 us -> 97.4 us
    pallas_call x1, Pallas kernels: 95.8 us -> 93 us  [per_device(): pl.pallas_call(chain_kernel, out_shape=[vm((HU, D), f32), vm((HP, 256), b...]
where the time goes in v4:
time: 100 us; the launch traced here: 99.9 us
  Pallas kernels  97.4 us (97%)
  between operations  1.47 us (1%)
    pallas_call x1, Pallas kernels, per_device(): pl.pallas_call(chain_kernel, out_shape=[vm((HU, D), f32), vm((HP, 256), b...  93 us
    pallas_call x1, Pallas kernels, per_device(): pl.pallas_call(place_kernel, out_shape=[jax.ShapeDtypeStruct((1, HU, D),...  4.4 us

profile of v4, /device:TPU:0, one launch (start us, length us, event | category | flops | bytes accessed | tf_op | source)
XLA Modules:
  0.0 99.9 jit_solution(5362611786628149569)
XLA Ops:
  1.4 0.1 pad.2.clone
  1.5 0.1 pad.3.clone
  1.6 0.1 fusion.4
  1.7 0.1 fusion.2
  1.8 0.7 maximum_maximum_fusion.vec_ref
  2.5 93.0 %chain.1 = (f32[216,5120]{1,0:T(8,128)S(1)}, bf16[256,256]{1,0:T(8,128)(2,1)S(1)}, bf16[256,5120]{1,0:T(8,128)(2,1)S(1)}, f32[32,5120]{1,0:T(8,128)S(1)}, f32[8,256]{1,0:T(8,128)S(1)}) custom-call(bf16[1,216,5120]{2,1,0:T(8,128)(2,1)} %up_ref.1, bf16[1,216,5120]{2,1,0:T(8,128)(2,1)} %down_ref.1, bf16[32,5120]{1,0:T(8,128)(2,1)} %nin_hbm.1, ...), custom_call_target="tpu_custom_call" | custom-call | tf_op jit(solution)/shard_map/chain/pallas_call | solution.py:706
  95.5 4.4 %place.1 = (f32[1,216,5120]{2,1,0:T(8,128)}, f32[1,216,5120]{2,1,0:T(8,128)}, f32[32,5120]{1,0:T(8,128)}, f32[5,1,160]{2,1,0:T(1,128)}) custom-call(f32[216,5120]{1,0:T(8,128)S(1)} %get-tuple-element.13.gu, bf16[256,256]{1,0:T(8,128)(2,1)S(1)} %get-tuple-element.14.at, bf16[256,5120]{1,0:T(8,128)(2,1)S(1)} %get-tuple-element.15.dz, ...), custom_call_target="tpu_custom_call" | custom-call | tf_op jit(solution)/shard_map/place/pallas_call | solution.py:723
  (2 shorter events, 0.0 us)

commit v5 on v4

--- a/solution.py
+++ b/solution.py
@@ -24,17 +24,14 @@
 NT = (((1,), (1,)), ((), ()))
 FAR = (2, 1, 3)
 
-def embedding(step_value, feature_width):
-    half_width = feature_width // 2
-    freqs = jnp.exp(-math.log(10000.0) * jnp.arange(half_width, dtype=f32) / half_width)
-    angles = step_value * freqs
-    return jnp.concatenate([jnp.cos(angles), jnp.sin(angles)], axis=-1)
 
 def device(x, y, z, c):
     return (y, lax.rem(x, 2) * 4 + z, lax.div(x, 2) * 2 + c)
 
+
 def turn(value, steps):
     return lax.rem(value + (steps % 4), 4)
+
 
 def gelu_parts(h):
     k = math.sqrt(2.0 / math.pi)
@@ -43,10 +40,11 @@
     slope = 0.5 * (1.0 + t) + 0.5 * h * (1.0 - t * t) * (k * (1.0 + 3.0 * 0.044715 * (h * h)))
     return value, slope
 
+
 def chain_kernel(
-    up_ref, down_ref, nin_hbm, noi_hbm, vec_ref, par_hbm,
+    up_ref, down_ref, nin_hbm, noi_hbm, time_ref, par_hbm,
     GU, at, DZ, score_out, small_out,
-    nin_ref, noi_ref, uu, par_ref, PR, dht, IV, U, UT, W, E, G1, G2A, G2B, DX, XH, H, HS, act, DA, dhb,
+    vec_ref, nin_ref, noi_ref, uu, par_ref, PR, dht, IV, U, UT, W, E, G1, G2A, G2B, DX, XH, H, HS, act, DA, dhb,
     zsA, zsB, rsA, rsB, sf, ss2, r2, Z, yS, yF, X0, Dv, CS, SM, T, T16, TX, T3, TZ,
     loc, wss, wrs, es, er,
     a1s, a1r, a2s, a2r, b1s, b1r, b2s, b2r,
@@ -155,7 +153,7 @@
         B.second(0)
 
     def gather_forward(A, B):
-        for d in FAR:
+        for d in (1, 3, 2):
             A.wait1(d)
             A.second(d)
             B.wait1(d)
@@ -197,6 +195,16 @@
         PR[j : j + 1, :] = par_ref[j, pl.ds(role, 1), :]
     PR[5:6, :] = par_ref[4, 0:1, :]
     PR[6:7, :] = par_ref[4, 1:2, :]
+
+    step_value = time_ref[0].astype(f32)
+    lane = lax.broadcasted_iota(jnp.int32, (2, D // 2), 1).astype(f32)
+    row = lax.broadcasted_iota(jnp.int32, (2, D // 2), 0)
+    angles = jnp.where(row == 0, gen_time, step_value) * jnp.exp(-math.log(10000.0) * lane / (D // 2))
+    vec_ref[0:2, 0 : D // 2] = jnp.cos(angles)
+    vec_ref[0:2, D // 2 : D] = jnp.sin(angles)
+    turn_angle = jnp.full((1, 128), 0.5 * math.pi, f32) * step_value / 1000.0
+    vec_ref[2:3, :] = jnp.broadcast_to(jnp.cos(turn_angle)[:, 0:1], (1, D))
+    vec_ref[3:4, :] = jnp.broadcast_to(jnp.sin(turn_angle)[:, 0:1], (1, D))
 
     @pl.when(is_gen)
     def _():
@@ -278,12 +286,11 @@
             norm_rows(zz, i)
             return carry
 
-        lax.fori_loop(0, 2, both, 0)
+        lax.fori_loop(0, 2, both, 0, unroll=True)
 
     arrived(UT.at[1], wrs.at[0])
     for s in range(2):
         H[s, :, 0:HU] = jnp.dot(uu[0:128, :], UT[s], preferred_element_type=f32)
-
     for s in range(2):
         act[s] = gelu_parts(H[s])[0].astype(bf16)
     loads[1].wait()
@@ -339,21 +346,20 @@
                 for xh_ in range(2):
                     arrived(rsB.at[d - 1, pl.ds(2 * xh_, 2)], rsBr.at[d - 1, xh_])
 
-        def add(i, carry, p=p, zs=zs, rs=rs, first=first):
-            total = zs[first, i].astype(f32)
-            for d in range(3):
-                total += rs[d, i].astype(f32)
-            sf[p, i] = total
-            ss2[p, i] = total.astype(bf16)
-            return carry
-
-        lax.fori_loop(0, 4, add, 0)
-        for d in FAR:
-            send(ss2.at[p, turn(second, d)], r2.at[p, d - 1], rs2s.at[p, d - 1], rs2r.at[p, d - 1], peer(d))
+        for d in FAR + (0,):
+            to = turn(second, d)
+            total = zs[first, to].astype(f32)
+            for k in range(3):
+                total += rs[k, to].astype(f32)
+            if d == 0:
+                sf[p] = total
+            else:
+                ss2[p, to] = total.astype(bf16)
+                send(ss2.at[p, to], r2.at[p, d - 1], rs2s.at[p, d - 1], rs2r.at[p, d - 1], peer(d))
     for p, zs, rs, first, second, peer in parts:
         for d in FAR:
             arrived(r2.at[p, d - 1], rs2r.at[p, d - 1])
-        total = sf[p, second]
+        total = sf[p]
         for d in range(3):
             total += r2[p, d].astype(f32)
         Z[p] = total
@@ -395,16 +401,16 @@
         critic = ((fake - x0) * 0.125 * gate).astype(bf16)
         block = jnp.where(y == 2, critic, gap)
         if p == 0:
-            G2A[x, z, :, 0:PW] = block
+            G2A[x, z] = block
+            g2a.first()
         else:
-            G2B[x, z] = block
+            G2B[x, z, :, 0:PW] = block
     hi = dist.astype(bf16)
     mid = (dist - hi.astype(f32)).astype(bf16)
     low = (dist - hi.astype(f32) - mid.astype(f32)).astype(bf16)
     lane = lax.broadcasted_iota(jnp.int32, (RB, 128), 1)
     tile = jnp.where(lane == 0, hi.astype(f32), jnp.where(lane == 1, mid.astype(f32), low.astype(f32)))
-    G2A[x, z, :, PW:] = tile.astype(bf16)
-    g2a.first()
+    G2B[x, z, :, PW:] = tile.astype(bf16)
     g2b.first()
     g2a.second(0)
     g2b.second(0)
@@ -419,11 +425,11 @@
 
     def gap_piece(k, xl_, zz):
         col = 2 * (k // 2) + xl_
-        return G2A[col, zz, :, 0:PW] if k % 2 == 0 else G2B[col, zz]
+        return G2A[col, zz] if k % 2 == 0 else G2B[col, zz, :, 0:PW]
 
     def share(xl_, zz):
         def one(col):
-            tile = G2A[col, zz, :, PW:].astype(f32)
+            tile = G2B[col, zz, :, PW:].astype(f32)
             return (tile[0:1, 0:1] + tile[0:1, 1:2]) + tile[0:1, 2:3]
 
         return one(xl_) + one(2 + xl_)
@@ -447,10 +453,11 @@
             scaled_rows(zz, j)
             return carry
 
-        lax.fori_loop(0, 2, both, 0)
+        lax.fori_loop(0, 2, both, 0, unroll=True)
         rows = pl.ds(pl.multiple_of(zz * 32, 32), 32)
         orows = pl.ds(pl.multiple_of(128 + zz * 32, 32), 32)
         send(DZ.at[rows], DZ.at[orows], dzs.at[i], dzr.at[i], sib)
+
 
     for l in range(8):
         CS[0, l : l + 1, :] = jnp.broadcast_to(share(l % 2, l // 2), (1, 128))
@@ -621,6 +628,7 @@
     def _():
         sent(DX.at[0], dxs)
 
+
 def place_kernel(gu, at, dz, score, small, up_out, down_out, score_out, small_out, gd, sems, down_sems):
     cuts = ((0, 56), (56, 56), (112, 56), (168, 48))
     copies = [pltpu.make_async_copy(score, score_out, sems.at[0])]
@@ -640,22 +648,14 @@
     for cp in copies:
         cp.wait()
 
+
 def per_device(noise_in, noise, timesteps, up_weight, down_weight, small_params):
-    step_value = timesteps[0].astype(f32)
-    angle = 0.5 * math.pi * step_value / 1000.0
-    vec = jnp.stack(
-        [
-            embedding(jnp.float32(gen_time), D),
-            embedding(step_value, D),
-            jnp.full((D,), jnp.cos(angle)),
-            jnp.full((D,), jnp.sin(angle)),
-        ]
-    )
     dma = pltpu.SemaphoreType.DMA
     vm = pltpu.VMEM
     vmem = pl.BlockSpec(memory_space=pltpu.VMEM)
     hbm = pl.BlockSpec(memory_space=pl.ANY)
     scratch = [
+        vm((4, D), f32),
         vm((32, D), bf16),
         vm((32, D), bf16),
         vm((256, D), bf16),
@@ -668,8 +668,8 @@
         vm((2, HU, D), bf16),
         vm((2, 4, 1, D), f32),
         vm((2, 4, 4, RB, PW), bf16),
+        vm((4, 4, RB, PW), bf16),
         vm((4, 4, RB, PW + 128), bf16),
-        vm((4, 4, RB, PW), bf16),
         vm((2, 2, RB, PW), bf16),
         vm((256, D), bf16),
         vm((2, 128, HP), f32),
@@ -681,7 +681,7 @@
         vm((4, 4, RB, PW), bf16),
         vm((3, 4, RB, PW), bf16),
         vm((3, 4, RB, PW), bf16),
-        vm((2, 4, RB, PW), f32),
+        vm((2, RB, PW), f32),
         vm((2, 4, RB, PW), bf16),
         vm((2, 3, RB, PW), bf16),
         vm((2, RB, PW), f32),
@@ -712,14 +712,14 @@
             vm((32, D), f32),
             vm((8, 256), f32),
         ],
-        in_specs=[hbm, hbm, hbm, hbm, vmem, hbm],
+        in_specs=[hbm, hbm, hbm, hbm, pl.BlockSpec(memory_space=pltpu.SMEM), hbm],
         out_specs=[vmem] * 5,
         scratch_shapes=scratch,
         compiler_params=pltpu.CompilerParams(
             collective_id=0, has_side_effects=True, vmem_limit_bytes=52 * 2**20
         ),
         name="chain",
-    )(up_weight, down_weight, noise_in, noise, vec, jnp.transpose(small_params, (1, 0, 2)))
+    )(up_weight, down_weight, noise_in, noise, timesteps, jnp.transpose(small_params, (1, 0, 2)))
     up_grad, down_grad, score, small = pl.pallas_call(
         place_kernel,
         out_shape=[
@@ -735,6 +735,7 @@
         name="place",
     )(*parts)
     return (score, up_grad, down_grad, jnp.transpose(small, (1, 0, 2)))
+
 
 def solution(mesh):
     in_specs = (

time: 100 us -> 97.8 us (0.978)
  Pallas kernels: 97.4 us -> 96.4 us
where the time goes in v5:
time: 97.8 us; the launch traced here: 97.7 us
  Pallas kernels  96.4 us (99%)
  between operations  1.29 us (1%)
    pallas_call x1, Pallas kernels, per_device(): pl.pallas_call(chain_kernel, out_shape=[vm((HU, D), f32), vm((HP, 256), b...  92 us
    pallas_call x1, Pallas kernels, per_device(): pl.pallas_call(place_kernel, out_shape=[jax.ShapeDtypeStruct((1, HU, D),...  4.4 us

profile of v5, /device:TPU:0, one launch (start us, length us, event | category | flops | bytes accessed | tf_op | source)
XLA Modules:
  0.0 97.7 jit_solution(3892382433638384731)
XLA Ops:
  1.3 92.0 %chain.1 = (f32[216,5120]{1,0:T(8,128)S(1)}, bf16[256,256]{1,0:T(8,128)(2,1)S(1)}, bf16[256,5120]{1,0:T(8,128)(2,1)S(1)}, f32[32,5120]{1,0:T(8,128)S(1)}, f32[8,256]{1,0:T(8,128)S(1)}) custom-call(bf16[1,216,5120]{2,1,0:T(8,128)(2,1)} %up_ref.1, bf16[1,216,5120]{2,1,0:T(8,128)(2,1)} %down_ref.1, bf16[32,5120]{1,0:T(8,128)(2,1)} %nin_hbm.1, ...), custom_call_target="tpu_custom_call" | custom-call | tf_op jit(solution)/shard_map/chain/pallas_call | solution.py:706
  93.3 4.4 %place.1 = (f32[1,216,5120]{2,1,0:T(8,128)}, f32[1,216,5120]{2,1,0:T(8,128)}, f32[32,5120]{1,0:T(8,128)}, f32[5,1,160]{2,1,0:T(1,128)}) custom-call(f32[216,5120]{1,0:T(8,128)S(1)} %get-tuple-element.13.gu, bf16[256,256]{1,0:T(8,128)(2,1)S(1)} %get-tuple-element.14.at, bf16[256,5120]{1,0:T(8,128)(2,1)S(1)} %get-tuple-element.15.dz, ...), custom_call_target="tpu_custom_call" | custom-call | tf_op jit(solution)/shard_map/place/pallas_call | solution.py:723

commit v6 on v5

--- a/solution.py
+++ b/solution.py
@@ -44,7 +44,7 @@
 def chain_kernel(
     up_ref, down_ref, nin_hbm, noi_hbm, time_ref, par_hbm,
     GU, at, DZ, score_out, small_out,
-    vec_ref, nin_ref, noi_ref, uu, par_ref, PR, dht, IV, U, UT, W, E, G1, G2A, G2B, DX, XH, H, HS, act, DA, dhb,
+    vec_ref, nin_ref, noi_ref, uu, par_ref, PR, dht, IV, U, UT, W, E, G1, G2A, G2B, DX, XH, H, HS, SL, VA, act, DA, dhb,
     zsA, zsB, rsA, rsB, sf, ss2, r2, Z, yS, yF, X0, Dv, CS, SM, T, T16, TX, T3, TZ,
     loc, wss, wrs, es, er,
     a1s, a1r, a2s, a2r, b1s, b1r, b2s, b2r,
@@ -374,6 +374,11 @@
             gate = PR[4:5, own_cols(p)] + vec_ref[1:2, own_cols(p)]
             yF[y - 2, p] = (G1[p, x, z].astype(f32) + gate * total).astype(bf16)
             y_send(yF, y - 2, p, 1)
+
+    arrived(HS, xr.at[0])
+    for s in range(2):
+        value, slope = gelu_parts(H[0] if s == 0 else HS[...])
+        SL[s], VA[s] = slope, value
 
     @pl.when(is_gen)
     def _():
@@ -463,7 +468,6 @@
         CS[0, l : l + 1, :] = jnp.broadcast_to(share(l % 2, l // 2), (1, 128))
     send(CS.at[0], CS.at[1], scs.at[0], scr.at[0], sib)
     live = y < 3
-    arrived(HS, xr.at[0])
     for i, dz in enumerate((0, 1, 3, 2)):
         orows = pl.ds(pl.multiple_of(128 + turn(z, -dz) * 32, 32), 32)
         arrived(DZ.at[orows], dzr.at[i])
@@ -474,8 +478,7 @@
         IV[l * RB : (l + 1) * RB, :] = jnp.broadcast_to(inv, (RB, 256))
     for s in range(2):
         rows = slice(s * 128, (s + 1) * 128)
-        value, slope = gelu_parts(H[0] if s == 0 else HS[...])
-        dh = jnp.where(live, DA[rows, :] * slope * IV[...], 0.0)
+        dh = jnp.where(live, DA[rows, :] * SL[s] * IV[...], 0.0)
         DA[rows, :] = dh
         dhb[rows, :] = dh.astype(bf16)
 
@@ -503,23 +506,7 @@
         SM[3:4, cols] = (1.0 + PR[0:1, cols]) * rows[3] + PR[1:2, cols] * rows[2]
         return carry
 
-    lax.fori_loop(0, D // CW, small, 0)
-
-    own_row = pl.ds(z * 2 + xl, 1)
-    inv_own = (1.0 / ((CS[0, own_row, :] + CS[1, own_row, :]) / (32.0 * D) + epsilon_gap))[:, 0:1]
-
-    @pl.when(y == 2)
-    def _():
-        arrived(DX.at[1 - xh], dxr)
-        for k in range(4):
-            score_out[own_rows, k * PW : (k + 1) * PW] = DX[k // 2, k % 2].astype(f32) * inv_own
-
-    @pl.when(y != 2)
-    def _():
-        for k in range(4):
-            score_out[own_rows, k * PW : (k + 1) * PW] = gap_piece(k, xl, z).astype(f32) * inv_own
-
-    send(score_out.at[own_rows], score_out.at[own_rows], scs.at[1], scr.at[1], sib)
+    lax.fori_loop(0, D // CW, small, 0, unroll=True)
 
     own_row = pl.ds(z * 2 + xl, 1)
     inv_own = (1.0 / ((CS[0, own_row, :] + CS[1, own_row, :]) / (32.0 * D) + epsilon_gap))[:, 0:1]
@@ -540,15 +527,29 @@
         T[t_ % 2, (t_ // 2) * 2 + f_ // 4, row : row + 8] = window
 
     T16[...] = T[...].astype(bf16)
-    near = [(dx, dc) for dc in range(2) for dx in (0, 1, 3, 2) if dx + dc]
+    near = [(dx, dc) for dx in (2, 1, 3, 0) for dc in range(2) if dx + dc]
     for k, (dx, dc) in enumerate(near):
         c_ = c if dc == 0 else 1 - c
         send(T16.at[c_, turn(x, dx)], TX.at[k], t1s.at[k], t1r.at[k], device(turn(x, dx), y, z, c_))
 
+
+    @pl.when(y == 2)
+    def _():
+        arrived(DX.at[1 - xh], dxr)
+        for k in range(4):
+            score_out[own_rows, k * PW : (k + 1) * PW] = DX[k // 2, k % 2].astype(f32) * inv_own
+
+    @pl.when(y != 2)
+    def _():
+        for k in range(4):
+            score_out[own_rows, k * PW : (k + 1) * PW] = gap_piece(k, xl, z).astype(f32) * inv_own
+
+    send(score_out.at[own_rows], score_out.at[own_rows], scs.at[1], scr.at[1], sib)
+
     live_rows = jnp.where(live, IV[...], 0.0)
     for s in range(2):
         rows = slice(s * 128, (s + 1) * 128)
-        value = gelu_parts(H[0] if s == 0 else HS[...])[0]
+        value = VA[s]
         dht[:, rows] = DA[rows, :].T.astype(bf16)
         at[:, rows] = (value * live_rows).T.astype(bf16)
     arrived(uu.at[other], xr.at[1])
@@ -559,7 +560,7 @@
             out[:, cols] = jnp.dot(left[...], right[:, cols], preferred_element_type=f32)[0:HU]
             return carry
 
-        lax.fori_loop(0, D // CW, step, 0)
+        lax.fori_loop(0, D // CW, step, 0, unroll=True)
 
     product(dht, uu, GU)
     for k in range(7):
@@ -569,14 +570,14 @@
         total += TX[k].astype(f32)
     for z_ in range(4):
         T3[z_] = total[z_ * 8 : z_ * 8 + 8]
+    @pl.when(is_gen)
+    def _():
+        for k in range(4):
+            d = FAR + (0,)
+            send(T3.at[turn(z, d[k])], TZ.at[3 + k], t2s.at[3 + k], t2r.at[3 + k], device(x, twin, turn(z, d[k]), c))
+
     for k, d in enumerate(FAR):
         send(T3.at[turn(z, d)], TZ.at[k], t2s.at[k], t2r.at[k], zdev(d))
-
-    @pl.when(is_gen)
-    def _():
-        for k in range(4):
-            d = (0,) + FAR
-            send(T3.at[turn(z, d[k])], TZ.at[3 + k], t2s.at[3 + k], t2r.at[3 + k], device(x, twin, turn(z, d[k]), c))
 
     for k in range(3):
         arrived(TZ.at[k], t2r.at[k])
@@ -674,6 +675,8 @@
         vm((256, D), bf16),
         vm((2, 128, HP), f32),
         vm((128, HP), f32),
+        vm((2, 128, HP), f32),
+        vm((2, 128, HP), f32),
         vm((2, 128, HP), bf16),
         vm((256, HP), f32),
         vm((256, HP), bf16),

time: 97.8 us -> 97.4 us (level)
  no operation moved by 1% of the time
where the time goes in v6:
time: 97.4 us; the launch traced here: 97.3 us
  Pallas kernels  96 us (99%)
  between operations  1.29 us (1%)
    pallas_call x1, Pallas kernels, per_device(): pl.pallas_call(chain_kernel, out_shape=[vm((HU, D), f32), vm((HP, 256), b...  91.6 us
    pallas_call x1, Pallas kernels, per_device(): pl.pallas_call(place_kernel, out_shape=[jax.ShapeDtypeStruct((1, HU, D),...  4.4 us

profile of v6, /device:TPU:0, one launch (start us, length us, event | category | flops | bytes accessed | tf_op | source)
XLA Modules:
  0.0 97.3 jit_solution(4618998545634787094)
XLA Ops:
  1.3 91.6 %chain.1 = (f32[216,5120]{1,0:T(8,128)S(1)}, bf16[256,256]{1,0:T(8,128)(2,1)S(1)}, bf16[256,5120]{1,0:T(8,128)(2,1)S(1)}, f32[32,5120]{1,0:T(8,128)S(1)}, f32[8,256]{1,0:T(8,128)S(1)}) custom-call(bf16[1,216,5120]{2,1,0:T(8,128)(2,1)} %up_ref.1, bf16[1,216,5120]{2,1,0:T(8,128)(2,1)} %down_ref.1, bf16[32,5120]{1,0:T(8,128)(2,1)} %nin_hbm.1, ...), custom_call_target="tpu_custom_call" | custom-call | tf_op jit(solution)/shard_map/chain/pallas_call | solution.py:709
  92.9 4.4 %place.1 = (f32[1,216,5120]{2,1,0:T(8,128)}, f32[1,216,5120]{2,1,0:T(8,128)}, f32[32,5120]{1,0:T(8,128)}, f32[5,1,160]{2,1,0:T(1,128)}) custom-call(f32[216,5120]{1,0:T(8,128)S(1)} %get-tuple-element.13.gu, bf16[256,256]{1,0:T(8,128)(2,1)S(1)} %get-tuple-element.14.at, bf16[256,5120]{1,0:T(8,128)(2,1)S(1)} %get-tuple-element.15.dz, ...), custom_call_target="tpu_custom_call" | custom-call | tf_op jit(solution)/shard_map/place/pallas_call | solution.py:726

commit v7 on v6

--- a/solution.py
+++ b/solution.py
@@ -123,28 +123,35 @@
         def peer(self, ring, d):
             return xdev(d) if (self.order == "xz") == (ring == 1) else zdev(d)
 
-        def first(self):
+        def first(self, peers=FAR):
+            own = self.block(0, 0)
+            for d in peers:
+                send(own, own, self.sems[0].at[d - 1], self.sems[1].at[d - 1], self.peer(1, d))
+
+        def second(self, d1, peers=FAR):
+            b = self.block(d1, 0)
+            for d in peers:
+                send(b, b, self.sems[2].at[d1, d - 1], self.sems[3].at[d1, d - 1], self.peer(2, d))
+
+        def wait1(self, d1):
+            arrived(self.block(d1, 0), self.sems[1].at[d1 - 1])
+
+        def wait2(self, d1, d2):
+            arrived(self.block(d1, d2), self.sems[3].at[d1, d2 - 1])
+
+        def drain(self, halved=None):
             own = self.block(0, 0)
             for d in FAR:
-                send(own, own, self.sems[0].at[d - 1], self.sems[1].at[d - 1], self.peer(1, d))
-
-        def second(self, d1):
-            b = self.block(d1, 0)
-            for d in FAR:
-                send(b, b, self.sems[2].at[d1, d - 1], self.sems[3].at[d1, d - 1], self.peer(2, d))
-
-        def wait1(self, d1):
-            arrived(self.block(d1, 0), self.sems[1].at[d1 - 1])
-
-        def wait2(self, d1, d2):
-            arrived(self.block(d1, d2), self.sems[3].at[d1, d2 - 1])
-
-        def drain(self):
-            own = self.block(0, 0)
-            for d in FAR:
-                sent(own, self.sems[0].at[d - 1])
-                for d1 in range(4):
-                    sent(own, self.sems[2].at[d1, d - 1])
+                for d1 in range(-1, 4):
+                    sem = self.sems[0].at[d - 1] if d1 < 0 else self.sems[2].at[d1, d - 1]
+                    if halved is not None and d == 2 and d1 == (-1 if self.order == "xz" else 0):
+
+                        @pl.when(jnp.logical_not(halved))
+                        def _(sem=sem):
+                            sent(own, sem)
+
+                    else:
+                        sent(own, sem)
 
     def gather_start(A, B):
         A.first()
@@ -178,7 +185,13 @@
     def _():
         for p in range(2):
             G1[p, x, z] = nin_ref[own_rows, own_cols(p)]
-        gather_start(g1a, g1b)
+            cols = pl.ds(pl.multiple_of((1 - xh) * (2 * PW) + p * PW, 128), PW)
+            G1[p, turn(x, 2), z] = nin_ref[own_rows, cols]
+        g1a.first((1, 3))
+        g1b.first()
+        g1a.second(0)
+        g1b.second(0, (1, 3))
+        g1a.second(2)
 
     loads[0].wait()
 
@@ -257,7 +270,19 @@
         g1a.second(0)
         g1b.second(0)
 
-    gather_forward(g1a, g1b)
+    for d in (1, 3):
+        g1a.wait1(d)
+        g1a.second(d)
+        g1b.wait1(d)
+        g1b.second(d)
+
+    @pl.when(jnp.logical_not(is_gen))
+    def _():
+        g1a.wait1(2)
+        g1a.second(2)
+
+    g1b.wait1(2)
+    g1b.second(2)
 
     def norm_rows(zz, xl_):
         rows = pl.ds(pl.multiple_of(zz * 32 + xl_ * RB, RB), RB)
@@ -279,7 +304,16 @@
             XH[rows, cols] = xhat.astype(bf16)
 
     for dz in (0, 1, 3, 2):
-        gather_group(g1a, g1b, dz)
+        if dz:
+            gather_group(g1a, g1b, dz)
+        else:
+            for d in (1, 3):
+                g1b.wait2(0, d)
+
+            @pl.when(jnp.logical_not(is_gen))
+            def _():
+                g1b.wait2(0, 2)
+
         zz = turn(z, -dz)
 
         def both(i, carry, zz=zz):
@@ -597,7 +631,9 @@
         sent(TX.at[k], t1s.at[k])
     for k in range(3):
         sent(TZ.at[k], t2s.at[k])
-    for g in (g1a, g1b, g2a, g2b):
+    for g in (g1a, g1b):
+        g.drain(is_gen)
+    for g in (g2a, g2b):
         g.drain()
     sent(UT.at[0], wss.at[0])
     sent(down_ref.at[0], wss.at[1])

time: 97.4 us -> 97.3 us (level)
  no operation moved by 1% of the time
where the time goes in v7:
time: 97.3 us; the launch traced here: 97.2 us
  Pallas kernels  95.9 us (99%)
  between operations  1.29 us (1%)
    pallas_call x1, Pallas kernels, per_device(): pl.pallas_call(chain_kernel, out_shape=[vm((HU, D), f32), vm((HP, 256), b...  91.5 us
    pallas_call x1, Pallas kernels, per_device(): pl.pallas_call(place_kernel, out_shape=[jax.ShapeDtypeStruct((1, HU, D),...  4.4 us

profile of v7, /device:TPU:0, one launch (start us, length us, event | category | flops | bytes accessed | tf_op | source)
XLA Modules:
  0.0 97.2 jit_solution(6714494486765933498)
XLA Ops:
  1.3 91.5 %chain.1 = (f32[216,5120]{1,0:T(8,128)S(1)}, bf16[256,256]{1,0:T(8,128)(2,1)S(1)}, bf16[256,5120]{1,0:T(8,128)(2,1)S(1)}, f32[32,5120]{1,0:T(8,128)S(1)}, f32[8,256]{1,0:T(8,128)S(1)}) custom-call(bf16[1,216,5120]{2,1,0:T(8,128)(2,1)} %up_ref.1, bf16[1,216,5120]{2,1,0:T(8,128)(2,1)} %down_ref.1, bf16[32,5120]{1,0:T(8,128)(2,1)} %nin_hbm.1, ...), custom_call_target="tpu_custom_call" | custom-call | tf_op jit(solution)/shard_map/chain/pallas_call | solution.py:745
  92.8 4.4 %place.1 = (f32[1,216,5120]{2,1,0:T(8,128)}, f32[1,216,5120]{2,1,0:T(8,128)}, f32[32,5120]{1,0:T(8,128)}, f32[5,1,160]{2,1,0:T(1,128)}) custom-call(f32[216,5120]{1,0:T(8,128)S(1)} %get-tuple-element.13.gu, bf16[256,256]{1,0:T(8,128)(2,1)S(1)} %get-tuple-element.14.at, bf16[256,5120]{1,0:T(8,128)(2,1)S(1)} %get-tuple-element.15.dz, ...), custom_call_target="tpu_custom_call" | custom-call | tf_op jit(solution)/shard_map/place/pallas_call | solution.py:762
